TPU v7x, 32 devices: a whole 2x2x4 slice. The times are simulated.
32 devices in a mesh: groups: 2 (over y), leaf: 4 (over z), rhs: 2 (over x), sub: 2 (over core).
Axes of the slice: x: 2, y: 2, z: 4, core: 2. Of those that a mesh axis runs over, the one named last changes fastest.
Arguments:
- densities: bfloat16 [64, 262144], P(None, ('groups', 'leaf', 'rhs', 'sub')), parts along dimension 1, may hold values from -6 to 6
- geometry: bfloat16 [4, 262144], P(None, ('groups', 'leaf', 'rhs', 'sub')), parts along dimension 1, may hold values from -0.31 to 1, as said below
- near_index: int32 [2048, 16], P(('groups', 'leaf', 'rhs', 'sub')), parts along dimension 0, may hold values from 0 to 1023, as said below
- leaf_basis: bfloat16 [2048, 32, 128], P(('groups', 'leaf', 'rhs', 'sub')), parts along dimension 0, may hold values from -0.5 to 0.5
- transfer_one: bfloat16 [512, 4, 32, 32], P(('groups', 'leaf', 'rhs', 'sub')), parts along dimension 0, may hold values from -0.75 to 0.75
- coupling_one: bfloat16 [512, 4, 32, 32], P(('groups', 'leaf', 'rhs', 'sub')), parts along dimension 0, may hold values from -0.375 to 0.375
- partners_one: int32 [512, 4], P(('groups', 'leaf', 'rhs', 'sub')), parts along dimension 0, may hold values from 0 to 255, as said below
- transfer_two: bfloat16 [128, 4, 32, 32], P(('groups', 'leaf', 'rhs', 'sub')), parts along dimension 0, may hold values from -0.75 to 0.75
- coupling_two: bfloat16 [128, 4, 32, 32], P(('groups', 'leaf', 'rhs', 'sub')), parts along dimension 0, may hold values from -0.25 to 0.25
- partners_two: int32 [128, 4], P(('groups', 'leaf', 'rhs', 'sub')), parts along dimension 0, may hold values from 0 to 63, as said below
- transfer_three: bfloat16 [32, 4, 32, 32], P(('groups', 'leaf', 'rhs', 'sub')), parts along dimension 0, may hold values from -0.75 to 0.75
- coupling_three: bfloat16 [32, 4, 32, 32], P(('groups', 'leaf', 'rhs', 'sub')), parts along dimension 0, may hold values from -0.1875 to 0.1875
- partners_three: int32 [32, 4], P(('groups', 'leaf', 'rhs', 'sub')), parts along dimension 0, may hold values from 0 to 15, as said below
- transfer_four: bfloat16 [8, 4, 32, 32], P('groups'), parts along dimension 0, may hold values from -0.75 to 0.75
- coupling_four: bfloat16 [8, 4, 32, 32], P('groups'), parts along dimension 0, may hold values from -0.125 to 0.125
- partners_four: int32 [8, 4], P('groups'), parts along dimension 0, may hold values from 0 to 3, as said below
Outputs:
- potential: bfloat16 [64, 262144], P(None, ('groups', 'leaf', 'rhs', 'sub')), parts along dimension 1
There are 2 independent parts, one for each index of `groups`. A program takes and returns all parts, laid end to end along the dimension named above; each array names one. Nothing has to cross between parts.
Inputs may be any that keep to these rules, and one draw needn't show every extreme that they name: `geometry`: rows a and the quadrature weights w lie in [0, 1] and [0.002, 0.02], y and z lie in [-0.31, 0.31] with y^2 + z^2 close to 0.09. `near_index`: entry 0 of leaf i is i; the other entries of a row are distinct leaves (i + o) mod 1024 with 1 <= |o| <= 16; some leaf lists both o = -16 and o = 16. `partners_one`: entry k of node n is (n + o) mod 256 with 1 <= |o| <= 16; entries may repeat; some node lists both extremes. `partners_two`: entry k of node n is (n + o) mod 64 with 1 <= |o| <= 4; entries may repeat; some node lists both extremes. `partners_three`: entry k of node n is (n + o) mod 16 with |o| = 1; entries may repeat. `partners_four`: entry k of node n is (n + o) mod 4 with 1 <= |o| <= 2; entries may repeat.
All inputs are finite; a program needn't handle non-finite values.
Results may differ from a plain program's by a relative error of at most 0.0056.
Values may be sent and summed in bfloat16 or wider, within the bound.
A program may use at most 64 MiB of HBM per device.

v0:
```python
import jax
import jax.numpy as jnp
from jax import lax
from jax.sharding import PartitionSpec as P

REACH = 16


spacing = 0.1
smoothing = 0.0025


def padded(cells, sides, width):
    for axis, dim in sides:
        count = lax.axis_size(axis)
        head = lax.slice_in_dim(cells, 0, width, axis=dim)
        tail = lax.slice_in_dim(cells, cells.shape[dim] - width, cells.shape[dim], axis=dim)
        cells = jnp.concatenate(
            [
                lax.ppermute(tail, axis, [(i, (i + 1) % count) for i in range(count)]),
                cells,
                lax.ppermute(head, axis, [((i + 1) % count, i) for i in range(count)]),
            ],
            axis=dim,
        )
    return cells


def kernel_block(target_geometry, source_geometry, offset):
    target = target_geometry.astype(jnp.float32)
    source = source_geometry.astype(jnp.float32)
    axial = spacing * (
        offset.astype(jnp.float32)[:, :, None, None]
        + source[0][:, :, None, :]
        - target[0][:, None, :, None]
    )
    across = source[1][:, :, None, :] - target[1][:, None, :, None]
    vertical = source[2][:, :, None, :] - target[2][:, None, :, None]
    distance = axial * axial + across * across + vertical * vertical + smoothing
    return (source[3][:, :, None, :] * lax.rsqrt(distance)).astype(jnp.bfloat16)


def lift_level(transfer, lower_coefs):
    node_total = transfer.shape[0]
    grouped = lower_coefs.reshape(node_total, 4, lower_coefs.shape[1], lower_coefs.shape[2])
    return jnp.einsum(
        "nqab,nqbr->nar", transfer, grouped, preferred_element_type=jnp.float32
    ).astype(jnp.bfloat16)


def lower_level(transfer, upper_grade):
    node_total = transfer.shape[0]
    spread = jnp.einsum("nqba,nbr->nqar", transfer, upper_grade, preferred_element_type=jnp.float32)
    return spread.reshape(node_total * 4, upper_grade.shape[1], upper_grade.shape[2])


def rim_level(coefficients):
    node_count = coefficients.shape[0]
    flattened = coefficients.reshape(node_count, -1)
    widened = padded(flattened, ((("leaf", "rhs", "sub"), 0),), node_count)
    return widened.reshape(3 * node_count, coefficients.shape[1], coefficients.shape[2])


def couple_local(coupling, partners, widened, shard_index, shards):
    node_count = coupling.shape[0]
    node_total = node_count * shards
    local_ids = jnp.arange(node_count, dtype=jnp.int32)
    own_nodes = shard_index * node_count + local_ids
    offset = (partners - own_nodes[:, None] + node_total // 2) % node_total - node_total // 2
    position = local_ids[:, None] + node_count + offset
    picked = widened[position]
    return jnp.einsum("nkab,nkbr->nar", coupling, picked, preferred_element_type=jnp.float32)


def couple_one(coupling, partners, coefficients, node_index):
    matrices = lax.dynamic_index_in_dim(coupling, node_index, 0, keepdims=False)
    partner_ids = lax.dynamic_index_in_dim(partners, node_index, 0, keepdims=False)
    picked = coefficients[partner_ids]
    return jnp.einsum("kab,kbr->ar", matrices, picked, preferred_element_type=jnp.float32)


def descend_one(transfer, upper_grade, node_index, child_index):
    rank_size = transfer.shape[2]
    matrix = lax.dynamic_slice(
        transfer, (node_index, child_index, 0, 0), (1, 1, rank_size, rank_size)
    )[0, 0]
    return jnp.einsum("ba,br->ar", matrix, upper_grade, preferred_element_type=jnp.float32)


def widen_near(densities, geometry, leaf_size):
    rhs_size = densities.shape[0]
    leaf_count = densities.shape[1] // leaf_size
    stacked = jnp.concatenate([densities, geometry], axis=0)
    widened = padded(stacked, ((("leaf", "rhs", "sub"), 1),), REACH * leaf_size)
    wide_leaves = widened.reshape(rhs_size + 4, leaf_count + 2 * REACH, leaf_size)
    return (wide_leaves[:rhs_size], wide_leaves[rhs_size:])


def near_blocks(
    block_starts,
    position,
    cycle_offset,
    own_geometry,
    source_dens_all,
    source_geometry_all,
    block_rows,
):

    def one_block(first_leaf):
        source_slots = lax.dynamic_slice_in_dim(position, first_leaf, block_rows, 0)
        block_offset = lax.dynamic_slice_in_dim(cycle_offset, first_leaf, block_rows, 0)
        target = lax.dynamic_slice_in_dim(own_geometry, first_leaf, block_rows, 1)
        kernel_vals = kernel_block(target, source_geometry_all[:, source_slots], block_offset)
        source_dens = source_dens_all[:, source_slots]
        return jnp.einsum(
            "rbks,bkts->rbt", source_dens, kernel_vals, preferred_element_type=jnp.float32
        )

    return lax.map(one_block, block_starts)


def body(
    densities,
    geometry,
    near_index,
    leaf_basis,
    transfer_one,
    coupling_one,
    partners_one,
    transfer_two,
    coupling_two,
    partners_two,
    transfer_three,
    coupling_three,
    partners_three,
    transfer_four,
    coupling_four,
    partners_four,
):
    shards = lax.axis_size(("leaf", "rhs", "sub"))
    shard_index = lax.axis_index(("leaf", "rhs", "sub"))
    leaf_count = leaf_basis.shape[0]
    rank_size = leaf_basis.shape[1]
    leaf_size = leaf_basis.shape[2]
    rhs_size = densities.shape[0]
    all_leaves = leaf_count * shards
    dens_leaves = densities.reshape(rhs_size, leaf_count, leaf_size)
    coef_zero = jnp.einsum(
        "nap,rnp->nar", leaf_basis, dens_leaves, preferred_element_type=jnp.float32
    ).astype(jnp.bfloat16)
    coef_one = lift_level(transfer_one, coef_zero)
    coef_two = lift_level(transfer_two, coef_one)
    coef_three = lift_level(transfer_three, coef_two)
    level_coefs = (coef_one, coef_two, coef_three)
    extended = [rim_level(coefs_one) for coefs_one in level_coefs]
    field_one = couple_local(coupling_one, partners_one, extended[0], shard_index, shards)
    field_two = couple_local(coupling_two, partners_two, extended[1], shard_index, shards)
    field_three = couple_local(coupling_three, partners_three, extended[2], shard_index, shards)
    flat_three = coef_three.reshape(1, -1)
    gathered = lax.all_gather(flat_three, ("leaf", "rhs", "sub"), axis=0, tiled=True)
    coef_four = lift_level(transfer_four, gathered.reshape(shards, rank_size, rhs_size))
    node_four = shard_index // 4
    grade_four = couple_one(coupling_four, partners_four, coef_four, node_four).astype(jnp.bfloat16)
    grade_three = (
        field_three[0] + descend_one(transfer_four, grade_four, node_four, shard_index % 4)
    ).astype(jnp.bfloat16)
    grade_two = (field_two + lower_level(transfer_three, grade_three[None])).astype(jnp.bfloat16)
    grade_one = (field_one + lower_level(transfer_two, grade_two)).astype(jnp.bfloat16)
    grade_zero = lower_level(transfer_one, grade_one).astype(jnp.bfloat16)
    far_field = jnp.einsum(
        "nar,nap->rnp", grade_zero, leaf_basis, preferred_element_type=jnp.float32
    )
    own_geometry = geometry.reshape(4, leaf_count, leaf_size)
    local_ids = jnp.arange(leaf_count, dtype=jnp.int32)
    own_leaves = shard_index * leaf_count + local_ids
    cycle_offset = (
        near_index - own_leaves[:, None] + all_leaves // 2
    ) % all_leaves - all_leaves // 2
    position = local_ids[:, None] + REACH + cycle_offset
    block_rows = 8
    wide_dens, wide_geometry = widen_near(densities, geometry, leaf_size)
    block_starts = jnp.arange(leaf_count // block_rows, dtype=jnp.int32) * block_rows
    block_terms = near_blocks(
        block_starts, position, cycle_offset, own_geometry, wide_dens, wide_geometry, block_rows
    )
    near_field = jnp.moveaxis(block_terms, 0, 1).reshape(rhs_size, leaf_count, leaf_size)
    return (near_field + far_field).astype(jnp.bfloat16).reshape(rhs_size, leaf_count * leaf_size)


def solution(mesh):
    in_specs = (
        P(None, ("groups", "leaf", "rhs", "sub")),
        P(None, ("groups", "leaf", "rhs", "sub")),
        P(("groups", "leaf", "rhs", "sub"), None),
        P(("groups", "leaf", "rhs", "sub"), None, None),
        P(("groups", "leaf", "rhs", "sub"), None, None, None),
        P(("groups", "leaf", "rhs", "sub"), None, None, None),
        P(("groups", "leaf", "rhs", "sub"), None),
        P(("groups", "leaf", "rhs", "sub"), None, None, None),
        P(("groups", "leaf", "rhs", "sub"), None, None, None),
        P(("groups", "leaf", "rhs", "sub"), None),
        P(("groups", "leaf", "rhs", "sub"), None, None, None),
        P(("groups", "leaf", "rhs", "sub"), None, None, None),
        P(("groups", "leaf", "rhs", "sub"), None),
        P("groups", None, None, None),
        P("groups", None, None, None),
        P("groups", None),
    )
    out_specs = P(None, ("groups", "leaf", "rhs", "sub"))
    return jax.shard_map(body, mesh=mesh, in_specs=in_specs, out_specs=out_specs, check_vma=False)
```

profile of v0, /device:TPU:0, one launch (start us, length us, event | category | flops | bytes accessed | tf_op | source)
XLA Modules:
  0.0 167.8 jit_solution(5451867175253574404)
XLA Ops:
  0.0 1.2 copy-done
  1.3 1.9 %convolution_convert_fusion = bf16[64,32,64]{2,1,0:T(8,128)(2,1)S(1)} fusion(bf16[64,32,128]{2,1,0:T(8,128)(2,1)S(1)} %copy-done, bf16[64,8192]{1,0:T(8,128)(2,1)} %param.18), kind=kOutput, calls=%fused_computation.28 | convolution fusion | flops 33685504 | bytes 1835008 | tf_op jit(solution)/shard_map/nap,rnp->nar/dot_general | solution.py:148
  5.1 5.0 %collective-permute-start.7 = (bf16[1,2048]{1,0:T(2,128)(2,1)}, bf16[1,2048]{1,0:T(2,128)(2,1)}, u32[]{:S(2)}, u32[]{:S(2)}) collective-permute-start(bf16[1,2048]{1,0:T(2,128)(2,1)} %reshape.156), channel_id=1, source_target_pairs={{1,0},{2,1},{3,2},{4,3},{5,4},{6,5},{7,6},{8,7},{9,8},{10,9},{11,1... | collective-permute-start | bytes 12296 | tf_op jit(solution)/shard_map/ppermute | solution.py:22
  10.8 4.4 %collective-permute-start.5 = (bf16[4,2048]{1,0:T(4,128)(2,1)}, bf16[4,2048]{1,0:T(4,128)(2,1)}, u32[]{:S(2)}, u32[]{:S(2)}) collective-permute-start(bf16[4,2048]{1,0:T(4,128)(2,1)} %reshape.154), channel_id=1, source_target_pairs={{1,0},{2,1},{3,2},{4,3},{5,4},{6,5},{7,6},{8,7},{9,8},{10,9},{11,1... | collective-permute-start | bytes 49160 | tf_op jit(solution)/shard_map/ppermute | solution.py:22
  16.9 18.4 %all-gather = bf16[16,1,2048]{2,1,0:T(2,128)(2,1)S(1)} all-gather(bf16[1,1,2048]{2,1,0:T(2,128)(2,1)S(1)} %reshape.220), channel_id=1, replica_groups=mesh['groups'=2,'leaf'=4,'rhs'=2,'sub'=2] {'leaf','rhs','sub'}, dimensions={0}, use_global_device_ids=true | all-gather | bytes 69632 | tf_op jit(solution)/shard_map/all_gather | solution.py:160
  40.8 1.1 fusion.16
  45.5 1.2 collective-permute-start.3
  50.1 4.5 %collective-permute-start.1 = (bf16[68,2048]{1,0:T(8,128)(2,1)}, bf16[68,2048]{1,0:T(8,128)(2,1)}, u32[]{:S(2)}, u32[]{:S(2)}) collective-permute-start(bf16[68,2048]{1,0:T(8,128)(2,1)} %get-tuple-element.92), channel_id=1, source_target_pairs={{1,0},{2,1},{3,2},{4,3},{5,4},{6,5},{7,6},{8,7},{9,8},{10,9},{11,1... | collective-permute-start | bytes 835592 | tf_op jit(solution)/shard_map/ppermute | solution.py:22
  56.9 1.1 fusion.18
  57.9 1.0 concatenate.34
  59.2 1.4 gather_fusion.2
  60.7 1.8 %fusion.11 = f32[16,64,128]{1,2,0:S(1)} fusion(bf16[16,32,128]{1,2,0:T(8,128)(2,1)S(1)} %bitcast.222, f32[16,32,64]{2,1,0:T(8,128)} %bitcast.229, bf16[16,4,32,32]{3,2,1,0:T(8,128)(2,1)} %param.23, bf16[16,4,32,64]{3,2,1,0:T(8,128)(2,1)} %bitcast.223), kind=kOutput, calls=%fused_computation.34 | convolution fusion | flops 16842752 | bytes 1179648
  63.3 1.5 copy_bitcast_fusion
  65.7 98.9 %while.10 = (s32[]{:T(128)}, f32[8,64,8,128]{3,1,2,0:T(8,128)}, s32[8]{0:T(128)S(1)}, s32[64,16]{1,0:T(8,128)}, bf16[4,96,128]{2,0,1:T(4,128)(2,1)S(1)}, /*index...) while((s32[]{:T(128)}, f32[8,64,8,128]{3,1,2,0:T(8,128)}, ...), condition=%wide.region_1.2_spmd, body=%wide.region_0.1_spmd.sunk | while | flops 293688832 | bytes 8197795 | solution.py:119
  70.0 2.1 %gather_fusion = bf16[128,64,128]{2,1,0:T(8,128)(2,1)} fusion(bf16[64,96,128]{2,0,1:T(8,128)(2,1)S(1)} %get-tuple-element.197, s32[1024]{0:T(1024)S(1)} %pad_clamp_fusion.6), kind=kCustom, calls=%fused_computation.1.clone.1 | custom fusion | bytes 4194816 | tf_op jit(solution)/shard_map/while/body/eval_jaxpr/gather | solution.py:114
  72.2 5.9 %fusion.79 = f32[8,64,8,128]{3,1,2,0:T(8,128)} fusion(f32[8,64,8,128]{3,1,2,0:T(8,128)} %get-tuple-element.180, s32[]{:T(128)} %get-tuple-element.179, bf16[64,8,16,128]{3,0,2,1:T(8,128)(2,1)} %bitcast.215, f32[8,128]{1,0:T(8,128)S(1)} %get-tuple-element.160, f32[8,16,128]{2,1,0:T(8,128)S(1)} %bitcast.227, f32[8,128]{1,0:T(8,128)S(1)} %get-tuple-element.162, ...), kind=kOutput, calls=%fused_computation.9.clone.1 | convolution fusion | flops 293601280 | bytes 2634240 | tf_op jit(solution)/shard_map/while/body/eval_jaxpr/rbks,bkts->rbt/dot_general | solution.py:115
  82.4 2.1 %gather_fusion = bf16[128,64,128]{2,1,0:T(8,128)(2,1)} fusion(bf16[64,96,128]{2,0,1:T(8,128)(2,1)S(1)} %get-tuple-element.197, s32[1024]{0:T(1024)S(1)} %pad_clamp_fusion.6), kind=kCustom, calls=%fused_computation.1.clone.1 | custom fusion | bytes 4194816 | tf_op jit(solution)/shard_map/while/body/eval_jaxpr/gather | solution.py:114
  84.5 5.9 %fusion.79 = f32[8,64,8,128]{3,1,2,0:T(8,128)} fusion(f32[8,64,8,128]{3,1,2,0:T(8,128)} %get-tuple-element.180, s32[]{:T(128)} %get-tuple-element.179, bf16[64,8,16,128]{3,0,2,1:T(8,128)(2,1)} %bitcast.215, f32[8,128]{1,0:T(8,128)S(1)} %get-tuple-element.160, f32[8,16,128]{2,1,0:T(8,128)S(1)} %bitcast.227, f32[8,128]{1,0:T(8,128)S(1)} %get-tuple-element.162, ...), kind=kOutput, calls=%fused_computation.9.clone.1 | convolution fusion | flops 293601280 | bytes 2634240 | tf_op jit(solution)/shard_map/while/body/eval_jaxpr/rbks,bkts->rbt/dot_general | solution.py:115
  94.8 2.1 %gather_fusion = bf16[128,64,128]{2,1,0:T(8,128)(2,1)} fusion(bf16[64,96,128]{2,0,1:T(8,128)(2,1)S(1)} %get-tuple-element.197, s32[1024]{0:T(1024)S(1)} %pad_clamp_fusion.6), kind=kCustom, calls=%fused_computation.1.clone.1 | custom fusion | bytes 4194816 | tf_op jit(solution)/shard_map/while/body/eval_jaxpr/gather | solution.py:114
  96.9 5.9 %fusion.79 = f32[8,64,8,128]{3,1,2,0:T(8,128)} fusion(f32[8,64,8,128]{3,1,2,0:T(8,128)} %get-tuple-element.180, s32[]{:T(128)} %get-tuple-element.179, bf16[64,8,16,128]{3,0,2,1:T(8,128)(2,1)} %bitcast.215, f32[8,128]{1,0:T(8,128)S(1)} %get-tuple-element.160, f32[8,16,128]{2,1,0:T(8,128)S(1)} %bitcast.227, f32[8,128]{1,0:T(8,128)S(1)} %get-tuple-element.162, ...), kind=kOutput, calls=%fused_computation.9.clone.1 | convolution fusion | flops 293601280 | bytes 2634240 | tf_op jit(solution)/shard_map/while/body/eval_jaxpr/rbks,bkts->rbt/dot_general | solution.py:115
  107.1 2.1 %gather_fusion = bf16[128,64,128]{2,1,0:T(8,128)(2,1)} fusion(bf16[64,96,128]{2,0,1:T(8,128)(2,1)S(1)} %get-tuple-element.197, s32[1024]{0:T(1024)S(1)} %pad_clamp_fusion.6), kind=kCustom, calls=%fused_computation.1.clone.1 | custom fusion | bytes 4194816 | tf_op jit(solution)/shard_map/while/body/eval_jaxpr/gather | solution.py:114
  109.3 5.9 %fusion.79 = f32[8,64,8,128]{3,1,2,0:T(8,128)} fusion(f32[8,64,8,128]{3,1,2,0:T(8,128)} %get-tuple-element.180, s32[]{:T(128)} %get-tuple-element.179, bf16[64,8,16,128]{3,0,2,1:T(8,128)(2,1)} %bitcast.215, f32[8,128]{1,0:T(8,128)S(1)} %get-tuple-element.160, f32[8,16,128]{2,1,0:T(8,128)S(1)} %bitcast.227, f32[8,128]{1,0:T(8,128)S(1)} %get-tuple-element.162, ...), kind=kOutput, calls=%fused_computation.9.clone.1 | convolution fusion | flops 293601280 | bytes 2634240 | tf_op jit(solution)/shard_map/while/body/eval_jaxpr/rbks,bkts->rbt/dot_general | solution.py:115
  119.5 2.1 %gather_fusion = bf16[128,64,128]{2,1,0:T(8,128)(2,1)} fusion(bf16[64,96,128]{2,0,1:T(8,128)(2,1)S(1)} %get-tuple-element.197, s32[1024]{0:T(1024)S(1)} %pad_clamp_fusion.6), kind=kCustom, calls=%fused_computation.1.clone.1 | custom fusion | bytes 4194816 | tf_op jit(solution)/shard_map/while/body/eval_jaxpr/gather | solution.py:114
  121.6 5.9 %fusion.79 = f32[8,64,8,128]{3,1,2,0:T(8,128)} fusion(f32[8,64,8,128]{3,1,2,0:T(8,128)} %get-tuple-element.180, s32[]{:T(128)} %get-tuple-element.179, bf16[64,8,16,128]{3,0,2,1:T(8,128)(2,1)} %bitcast.215, f32[8,128]{1,0:T(8,128)S(1)} %get-tuple-element.160, f32[8,16,128]{2,1,0:T(8,128)S(1)} %bitcast.227, f32[8,128]{1,0:T(8,128)S(1)} %get-tuple-element.162, ...), kind=kOutput, calls=%fused_computation.9.clone.1 | convolution fusion | flops 293601280 | bytes 2634240 | tf_op jit(solution)/shard_map/while/body/eval_jaxpr/rbks,bkts->rbt/dot_general | solution.py:115
  131.9 2.1 %gather_fusion = bf16[128,64,128]{2,1,0:T(8,128)(2,1)} fusion(bf16[64,96,128]{2,0,1:T(8,128)(2,1)S(1)} %get-tuple-element.197, s32[1024]{0:T(1024)S(1)} %pad_clamp_fusion.6), kind=kCustom, calls=%fused_computation.1.clone.1 | custom fusion | bytes 4194816 | tf_op jit(solution)/shard_map/while/body/eval_jaxpr/gather | solution.py:114
  134.0 5.9 %fusion.79 = f32[8,64,8,128]{3,1,2,0:T(8,128)} fusion(f32[8,64,8,128]{3,1,2,0:T(8,128)} %get-tuple-element.180, s32[]{:T(128)} %get-tuple-element.179, bf16[64,8,16,128]{3,0,2,1:T(8,128)(2,1)} %bitcast.215, f32[8,128]{1,0:T(8,128)S(1)} %get-tuple-element.160, f32[8,16,128]{2,1,0:T(8,128)S(1)} %bitcast.227, f32[8,128]{1,0:T(8,128)S(1)} %get-tuple-element.162, ...), kind=kOutput, calls=%fused_computation.9.clone.1 | convolution fusion | flops 293601280 | bytes 2634240 | tf_op jit(solution)/shard_map/while/body/eval_jaxpr/rbks,bkts->rbt/dot_general | solution.py:115
  144.2 2.1 %gather_fusion = bf16[128,64,128]{2,1,0:T(8,128)(2,1)} fusion(bf16[64,96,128]{2,0,1:T(8,128)(2,1)S(1)} %get-tuple-element.197, s32[1024]{0:T(1024)S(1)} %pad_clamp_fusion.6), kind=kCustom, calls=%fused_computation.1.clone.1 | custom fusion | bytes 4194816 | tf_op jit(solution)/shard_map/while/body/eval_jaxpr/gather | solution.py:114
  146.4 5.9 %fusion.79 = f32[8,64,8,128]{3,1,2,0:T(8,128)} fusion(f32[8,64,8,128]{3,1,2,0:T(8,128)} %get-tuple-element.180, s32[]{:T(128)} %get-tuple-element.179, bf16[64,8,16,128]{3,0,2,1:T(8,128)(2,1)} %bitcast.215, f32[8,128]{1,0:T(8,128)S(1)} %get-tuple-element.160, f32[8,16,128]{2,1,0:T(8,128)S(1)} %bitcast.227, f32[8,128]{1,0:T(8,128)S(1)} %get-tuple-element.162, ...), kind=kOutput, calls=%fused_computation.9.clone.1 | convolution fusion | flops 293601280 | bytes 2634240 | tf_op jit(solution)/shard_map/while/body/eval_jaxpr/rbks,bkts->rbt/dot_general | solution.py:115
  156.6 2.1 %gather_fusion = bf16[128,64,128]{2,1,0:T(8,128)(2,1)} fusion(bf16[64,96,128]{2,0,1:T(8,128)(2,1)S(1)} %get-tuple-element.197, s32[1024]{0:T(1024)S(1)} %pad_clamp_fusion.6), kind=kCustom, calls=%fused_computation.1.clone.1 | custom fusion | bytes 4194816 | tf_op jit(solution)/shard_map/while/body/eval_jaxpr/gather | solution.py:114
  158.7 5.9 %fusion.79 = f32[8,64,8,128]{3,1,2,0:T(8,128)} fusion(f32[8,64,8,128]{3,1,2,0:T(8,128)} %get-tuple-element.180, s32[]{:T(128)} %get-tuple-element.179, bf16[64,8,16,128]{3,0,2,1:T(8,128)(2,1)} %bitcast.215, f32[8,128]{1,0:T(8,128)S(1)} %get-tuple-element.160, f32[8,16,128]{2,1,0:T(8,128)S(1)} %bitcast.227, f32[8,128]{1,0:T(8,128)S(1)} %get-tuple-element.162, ...), kind=kOutput, calls=%fused_computation.9.clone.1 | convolution fusion | flops 293601280 | bytes 2634240 | tf_op jit(solution)/shard_map/while/body/eval_jaxpr/rbks,bkts->rbt/dot_general | solution.py:115
  164.6 2.1 %fusion.7 = bf16[64,8,8,128]{3,2,1,0:T(8,128)(2,1)S(1)} fusion(bf16[64,32,64]{2,1,0:T(8,128)(2,1)S(1)} %bitcast.225, bf16[64,32,128]{2,1,0:T(8,128)(2,1)S(1)} %copy-done, f32[8,64,8,128]{3,1,2,0:T(8,128)} %get-tuple-element.47), kind=kOutput, calls=%fused_computation.27 | convolution fusion | flops 34603008 | bytes 3932160 | tf_op jit(solution)/shard_map/nar,nap->rnp/dot_general | solution.py:170
  166.7 1.2 copy.64
  (168 shorter events, 40.5 us)
Async XLA Ops:
  0.0 1.3 copy-start
  0.0 16.1 %copy-start.1 = (bf16[64,8192]{1,0:T(8,128)(2,1)S(1)}, bf16[64,8192]{1,0:T(8,128)(2,1)}, u32[]{:S(2)}) copy-start(bf16[64,8192]{1,0:T(8,128)(2,1)} %param.18) | copy-start | bytes 3145732
  0.0 3.1 %copy-start.2 = (bf16[16,4,32,32]{3,2,1,0:T(8,128)(2,1)S(1)}, bf16[16,4,32,32]{3,2,1,0:T(8,128)(2,1)}, u32[]{:S(2)}) copy-start(bf16[16,4,32,32]{3,2,1,0:T(8,128)(2,1)} %param.22) | copy-start | bytes 393220
  0.0 3.5 %copy-start.5 = (bf16[4,4,32,32]{3,2,1,0:T(8,128)(2,1)S(1)}, bf16[4,4,32,32]{3,2,1,0:T(8,128)(2,1)}, u32[]{:S(2)}) copy-start(bf16[4,4,32,32]{3,2,1,0:T(8,128)(2,1)} %param.25) | copy-start | bytes 98308
  0.0 3.7 %copy-start.9 = (bf16[1,4,32,32]{3,2,1,0:T(8,128)(2,1)S(1)}, bf16[1,4,32,32]{3,2,1,0:T(8,128)(2,1)}, u32[]{:S(2)}) copy-start(bf16[1,4,32,32]{3,2,1,0:T(8,128)(2,1)} %param.28) | copy-start | bytes 24580
  3.7 12.3 %copy-start.6 = (bf16[4,32,64]{2,1,0:T(8,128)(2,1)}, bf16[4,32,64]{2,1,0:T(8,128)(2,1)S(1)}, u32[]{:S(2)}) copy-start(bf16[4,32,64]{2,1,0:T(8,128)(2,1)S(1)} %fusion.17) | copy-start | bytes 49156
  4.6 40.8 %collective-permute-start.6 = (bf16[1,2048]{1,0:T(2,128)(2,1)}, bf16[1,2048]{1,0:T(2,128)(2,1)}, u32[]{:S(2)}, u32[]{:S(2)}) collective-permute-start(bf16[1,2048]{1,0:T(2,128)(2,1)} %reshape.156), channel_id=1, source_target_pairs={{0,1},{1,2},{2,3},{3,4},{4,5},{5,6},{6,7},{7,8},{8,9},{9,10},{10,1... | collective-permute-start | bytes 12296 | tf_op jit(solution)/shard_map/ppermute | solution.py:20
  5.1 42.4 %collective-permute-start.7 = (bf16[1,2048]{1,0:T(2,128)(2,1)}, bf16[1,2048]{1,0:T(2,128)(2,1)}, u32[]{:S(2)}, u32[]{:S(2)}) collective-permute-start(bf16[1,2048]{1,0:T(2,128)(2,1)} %reshape.156), channel_id=1, source_target_pairs={{1,0},{2,1},{3,2},{4,3},{5,4},{6,5},{7,6},{8,7},{9,8},{10,9},{11,1... | collective-permute-start | bytes 12296 | tf_op jit(solution)/shard_map/ppermute | solution.py:22
  10.8 39.3 %collective-permute-start.4 = (bf16[4,2048]{1,0:T(4,128)(2,1)}, bf16[4,2048]{1,0:T(4,128)(2,1)}, u32[]{:S(2)}, u32[]{:S(2)}) collective-permute-start(bf16[4,2048]{1,0:T(4,128)(2,1)} %reshape.154), channel_id=1, source_target_pairs={{0,1},{1,2},{2,3},{3,4},{4,5},{5,6},{6,7},{7,8},{8,9},{9,10},{10,1... | collective-permute-start | bytes 49160 | tf_op jit(solution)/shard_map/ppermute | solution.py:20
  10.8 44.7 %collective-permute-start.5 = (bf16[4,2048]{1,0:T(4,128)(2,1)}, bf16[4,2048]{1,0:T(4,128)(2,1)}, u32[]{:S(2)}, u32[]{:S(2)}) collective-permute-start(bf16[4,2048]{1,0:T(4,128)(2,1)} %reshape.154), channel_id=1, source_target_pairs={{1,0},{2,1},{3,2},{4,3},{5,4},{6,5},{7,6},{8,7},{9,8},{10,9},{11,1... | collective-permute-start | bytes 49160 | tf_op jit(solution)/shard_map/ppermute | solution.py:22
  16.0 41.9 %collective-permute-start.2 = (bf16[16,2048]{1,0:T(8,128)(2,1)}, bf16[16,2048]{1,0:T(8,128)(2,1)}, u32[]{:S(2)}, u32[]{:S(2)}) collective-permute-start(bf16[16,2048]{1,0:T(8,128)(2,1)} %reshape.152), channel_id=1, source_target_pairs={{0,1},{1,2},{2,3},{3,4},{4,5},{5,6},{6,7},{7,8},{8,9},{9,10},{10,1... | collective-permute-start | bytes 196616 | tf_op jit(solution)/shard_map/ppermute | solution.py:20
  16.2 29.2 %copy-start.10 = (bf16[1,4,32,32]{3,2,1,0:T(8,128)(2,1)S(1)}, bf16[1,4,32,32]{3,2,1,0:T(8,128)(2,1)}, u32[]{:S(2)}) copy-start(bf16[1,4,32,32]{3,2,1,0:T(8,128)(2,1)} %param.28) | copy-start | bytes 24580
  16.2 29.2 %copy-start.8 = (bf16[4,8192]{1,0:T(4,128)(2,1)S(1)}, bf16[4,8192]{1,0:T(4,128)(2,1)}, u32[]{:S(2)}) copy-start(bf16[4,8192]{1,0:T(4,128)(2,1)} %param.19) | copy-start | bytes 196612
  16.9 32.0 %copy-start.12 = (bf16[1,4,32,32]{3,2,1,0:T(8,128)(2,1)S(1)}, bf16[1,4,32,32]{3,2,1,0:T(8,128)(2,1)}, u32[]{:S(2)}) copy-start(bf16[1,4,32,32]{3,2,1,0:T(8,128)(2,1)} %param.29) | copy-start | bytes 24580
  35.6 20.6 %copy-start.7 = (bf16[4,32,64]{2,1,0:T(8,128)(2,1)S(1)}, bf16[4,32,64]{2,1,0:T(8,128)(2,1)}, u32[]{:S(2)}) copy-start(bf16[4,32,64]{2,1,0:T(8,128)(2,1)} %copy-done.6) | copy-start | bytes 49156
  39.2 17.6 %copy-start.11 = (bf16[4,4,32,32]{3,2,1,0:T(8,128)(2,1)S(1)}, bf16[4,4,32,32]{3,2,1,0:T(8,128)(2,1)}, u32[]{:S(2)}) copy-start(bf16[4,4,32,32]{3,2,1,0:T(8,128)(2,1)} %param.26) | copy-start | bytes 98308
  45.3 15.3 %copy-start.3 = (bf16[16,4,32,32]{2,3,1,0:T(8,128)(2,1)S(1)}, bf16[16,4,32,32]{2,3,1,0:T(8,128)(2,1)}, u32[]{:S(2)}) copy-start(bf16[16,4,32,32]{2,3,1,0:T(8,128)(2,1)} %copy.45) | copy-start | bytes 393220
  45.5 13.5 %collective-permute-start.3 = (bf16[16,2048]{1,0:T(8,128)(2,1)}, bf16[16,2048]{1,0:T(8,128)(2,1)S(1)}, u32[]{:S(2)}, u32[]{:S(2)}) collective-permute-start(bf16[16,2048]{1,0:T(8,128)(2,1)} %reshape.152), channel_id=1, source_target_pairs={{1,0},{2,1},{3,2},{4,3},{5,4},{6,5},{7,6},{8,7},{9,8},{10,9},{11,1... | collective-permute-start | bytes 196616 | tf_op jit(solution)/shard_map/ppermute | solution.py:22
  47.5 15.8 %collective-permute-start = (bf16[68,2048]{1,0:T(8,128)(2,1)}, bf16[68,2048]{1,0:T(8,128)(2,1)}, u32[]{:S(2)}, u32[]{:S(2)}) collective-permute-start(bf16[68,2048]{1,0:T(8,128)(2,1)} %get-tuple-element.91), channel_id=1, source_target_pairs={{0,1},{1,2},{2,3},{3,4},{4,5},{5,6},{6,7},{7,8},{8,9},{9,10},{10,1... | collective-permute-start | bytes 835592 | tf_op jit(solution)/shard_map/ppermute | solution.py:20
  50.1 13.2 %collective-permute-start.1 = (bf16[68,2048]{1,0:T(8,128)(2,1)}, bf16[68,2048]{1,0:T(8,128)(2,1)}, u32[]{:S(2)}, u32[]{:S(2)}) collective-permute-start(bf16[68,2048]{1,0:T(8,128)(2,1)} %get-tuple-element.92), channel_id=1, source_target_pairs={{1,0},{2,1},{3,2},{4,3},{5,4},{6,5},{7,6},{8,7},{9,8},{10,9},{11,1... | collective-permute-start | bytes 835592 | tf_op jit(solution)/shard_map/ppermute | solution.py:22
  65.6 99.0 %copy-start.4 = (bf16[16,64,4,32]{1,3,2,0:T(8,128)(2,1)S(1)}, bf16[16,64,4,32]{1,3,2,0:T(8,128)(2,1)}, u32[]{:S(2)}) copy-start(bf16[16,64,4,32]{1,3,2,0:T(8,128)(2,1)} %convert_element_type.77) | copy-start | bytes 786436
where the time goes:
time: 170 us; the launch traced here: 168 us
  matrix products  57.8 us (34%)
  local copies, waits for them, and re-layouts  44.9 us (26%)
  blocking collectives  18.4 us (11%)
  starting transfers between devices  15.6 us (9%)
  other arithmetic  15.5 us (9%)
  loops' own time  15.3 us (9%)
    dot_general x8, matrix products, one_block(): jnp.einsum('rbks,bkts->rbt', source_dens, kernel_vals, preferred_element_...  47 us
    all_gather x1, blocking collectives, body(): lax.all_gather(flat_three, ('leaf', 'rhs', 'sub'), axis=0, tiled=True)  18.4 us
    gather x8, local copies, waits for them, and re-layouts, one_block(): source_dens = source_dens_all[:, source_slots]  16.9 us
    another operation x1, loops' own time, near_blocks(): return lax.map(one_block, block_starts)  15.3 us
    ppermute x4, starting transfers between devices, padded(): lax.ppermute(head, axis, [((i + 1) % count, i) for i in range(count)])  15.1 us
    gather x8, local copies, waits for them, and re-layouts, one_block(): source_geometry_all[:, source_slots]  5.96 us
    select_n x8, other arithmetic, one_block(): source_geometry_all[:, source_slots]  5.8 us
    dynamic_slice x8, local copies, waits for them, and re-layouts, near_blocks(): return lax.map(one_block, block_starts)  4.75 us
  transfers between devices with their start and end apart: 8, of which 0 were waited for; matrix products, arithmetic and copies ran while one was open for 15% of the time, Pallas kernels for 0%

commit v1 on v0

v1 whole, which is shorter than its diff:
```python
import functools

import jax
import jax.numpy as jnp
from jax import lax
from jax.experimental import pallas as pl
from jax.experimental.pallas import tpu as pltpu
from jax.sharding import PartitionSpec as P

AXES = ("leaf", "rhs", "sub")
REACH = 16
SPACING2 = 0.01
SMOOTH = 0.0025
f32 = jnp.float32
bf16 = jnp.bfloat16


def dot(a, b, ca, cb):
    return lax.dot_general(a, b, (((ca,), (cb,)), ((), ())), preferred_element_type=f32)


def wrap(d, total):
    d = jnp.where(d >= total // 2, d - total, d)
    return jnp.where(d < -(total // 2), d + total, d)


def split3(v):
    hi = v.astype(bf16).astype(f32)
    r1 = v - hi
    mid = r1.astype(bf16).astype(f32)
    return r1, r1 - mid


def up_kernel(dens, basis, t1, t2, t3, out, c0):
    leaves = basis.shape[0]
    rank = basis.shape[1]
    n1, n2, n3 = t1.shape[0], t2.shape[0], t3.shape[0]
    for i in range(leaves):
        c0[i] = dot(basis[i], dens[:, i * 128 : (i + 1) * 128], 1, 1).astype(bf16)

    def lift(t, count, source, base, into):
        for n in range(count):
            acc = dot(t[n, 0], source[base + 4 * n], 1, 0)
            for q in range(1, 4):
                acc += dot(t[n, q], source[base + 4 * n + q], 1, 0)
            out[into + n] = acc.astype(bf16)

    lift(t1, n1, c0, 0, 0)
    lift(t2, n2, out, 0, n1)
    lift(t3, n3, out, n1, n1 + n2)


def near_kernel(shards, near_index, dens, geom, left, right, out, densw, fa, fb, tf):
    leaves = near_index.shape[0]
    near = near_index.shape[1]
    rhs = dens.shape[0]
    total = leaves * shards
    me = lax.axis_index(AXES)
    row8 = lax.broadcasted_iota(jnp.int32, (8, 128), 0)
    first = (row8 == 0) | (row8 == 3) | (row8 >= 6)
    second = (row8 == 1) | (row8 == 4)

    def prepare(slot, d, g, own):
        g = g.astype(f32)
        a, y, z, w = (g[r : r + 1] for r in range(4))
        densw[slot] = (d.astype(f32) * w).astype(bf16)
        a8, y8, z8 = (jnp.broadcast_to(v, (8, 128)) for v in (a, y, z))
        square = SPACING2 * a8 * a8 + y8 * y8 + z8 * z8
        fa[slot] = jnp.where(
            row8 < 3, square + SMOOTH,
            jnp.where(row8 < 6, (-2.0 * SPACING2) * a8, jnp.where(row8 == 6, -2.0 * y8, -2.0 * z8)),
        )
        fb[slot] = jnp.where(row8 < 3, (2.0 * SPACING2) * a8, jnp.where(row8 < 6, -2.0 * SPACING2, 0.0))
        if own:
            r1, r2 = split3(square)
            upper = jnp.where(row8 < 3, 1.0, jnp.where(row8 < 6, a8, jnp.where(row8 == 6, y8, z8)))
            lower = jnp.where(row8 == 0, square, jnp.where(row8 == 1, r1, jnp.where(row8 == 2, r2, 0.0)))
            tf[slot - REACH] = jnp.concatenate([upper, lower], axis=0).astype(bf16)

    for j in range(REACH):
        cols = slice(j * 128, (j + 1) * 128)
        prepare(j, left[:rhs, cols], left[rhs:, cols], False)
        prepare(REACH + leaves + j, right[:rhs, cols], right[rhs:, cols], False)
    for j in range(leaves):
        cols = slice(j * 128, (j + 1) * 128)
        prepare(REACH + j, dens[:, cols], geom[:, cols], True)

    quad = jnp.where(row8 < 3, SPACING2, 0.0)
    tail = jnp.where(row8 < 3, 1.0, 0.0)

    def source(i, k):
        o = wrap(near_index[i, k] - (me * leaves + i), total)
        pos = i + REACH + o
        of = o.astype(f32)
        v = fa[pos] + of * (fb[pos] + of * quad)
        r1, r2 = split3(v)
        x = jnp.where(first, v, jnp.where(second, r1, r2))
        return jnp.concatenate([x, tail], axis=0).astype(bf16), densw[pos]

    def one(i, carry):
        target = tf[i]
        acc = None
        for k in range(0, near, 2):
            x0, d0 = source(i, k)
            x1, d1 = source(i, k + 1)
            dist = dot(target, jnp.concatenate([x0, x1], axis=1), 0, 0)
            block = lax.rsqrt(dist.astype(bf16))
            term = dot(block, jnp.concatenate([d0, d1], axis=1), 1, 1)
            acc = term if acc is None else acc + term
        out[:, pl.ds(pl.multiple_of(i * 128, 128), 128)] = acc.T
        return carry

    lax.fori_loop(0, leaves, one, 0)


def down_kernel(
    shards, p1, p2, p3, p4, own, left, right, three, c1, c2, c3, c4, t1, t2, t3, t4, basis, nearf, out, wide
):
    n1, n2 = c1.shape[0], c2.shape[0]
    me = lax.axis_index(AXES)
    leaves = basis.shape[0]
    spans = ((0, n1), (n1, n2), (n1 + n2, 1))
    bases = (0, 3 * n1, 3 * (n1 + n2))
    for (lo, n), base in zip(spans, bases):
        for m in range(n):
            wide[base + m] = left[lo + m]
            wide[base + n + m] = own[lo + m]
            wide[base + 2 * n + m] = right[lo + m]

    def couple(c, p, level, n):
        count = spans[level][1]
        acc = None
        for k in range(4):
            o = wrap(p[n, k] - (me * count + n), count * shards)
            term = dot(c[n, k], wide[bases[level] + count + n + o], 1, 0)
            acc = term if acc is None else acc + term
        return acc

    node = me // 4
    field4 = None
    for k in range(4):
        q4 = p4[node, k]
        acc = None
        for q in range(4):
            term = dot(t4[q4, q], three[4 * q4 + q], 1, 0)
            acc = term if acc is None else acc + term
        term = dot(c4[node, k], acc.astype(bf16), 1, 0)
        field4 = term if field4 is None else field4 + term
    g4 = field4.astype(bf16)
    g3 = (couple(c3, p3, 2, 0) + dot(t4[node, me % 4], g4, 0, 0)).astype(bf16)
    for m in range(n2):
        g2 = (couple(c2, p2, 1, m) + dot(t3[0, m], g3, 0, 0)).astype(bf16)
        for q in range(4):
            n = 4 * m + q
            g1 = (couple(c1, p1, 0, n) + dot(t2[m, q], g2, 0, 0)).astype(bf16)
            for r in range(4):
                i = 4 * n + r
                g0 = dot(t1[n, r], g1, 0, 0).astype(bf16)
                far = dot(g0, basis[i], 0, 0)
                cols = slice(i * 128, (i + 1) * 128)
                out[:, cols] = (nearf[:, cols] + far).astype(bf16)


VM = pl.BlockSpec(memory_space=pltpu.VMEM)
SM = pl.BlockSpec(memory_space=pltpu.SMEM)


def shift(v, step):
    count = lax.axis_size(AXES)
    return lax.ppermute(v, AXES, [(i, (i + step) % count) for i in range(count)])


def body(
    densities, geometry, near_index, leaf_basis,
    transfer_one, coupling_one, partners_one,
    transfer_two, coupling_two, partners_two,
    transfer_three, coupling_three, partners_three,
    transfer_four, coupling_four, partners_four,
):
    shards = lax.axis_size(AXES)
    leaves, rank, _ = leaf_basis.shape
    rhs, points = densities.shape
    n1, n2 = transfer_one.shape[0], transfer_two.shape[0]
    nodes = n1 + n2 + 1
    params = pltpu.CompilerParams(vmem_limit_bytes=40 * 2**20)
    width = REACH * 128
    tail = jnp.concatenate([densities[:, points - width :], geometry[:, points - width :]], axis=0)
    head = jnp.concatenate([densities[:, :width], geometry[:, :width]], axis=0)
    left = shift(tail, 1)
    right = shift(head, -1)

    coefs = pl.pallas_call(
        up_kernel,
        out_shape=jax.ShapeDtypeStruct((nodes, rank, rhs), bf16),
        in_specs=[VM] * 5,
        out_specs=VM,
        scratch_shapes=[pltpu.VMEM((leaves, rank, rhs), bf16)],
        compiler_params=params,
        name="up",
        cost_estimate=pl.CostEstimate(flops=10**8, bytes_accessed=2 * 10**6, transcendentals=0),
    )(densities, leaf_basis, transfer_one, transfer_two, transfer_three)
    cleft = shift(coefs, 1)
    cright = shift(coefs, -1)
    three = lax.all_gather(coefs[nodes - 1].reshape(1, -1), AXES, axis=0, tiled=True)
    three = three.reshape(shards, rank, rhs)

    wide = leaves + 2 * REACH
    nearf = pl.pallas_call(
        functools.partial(near_kernel, shards),
        out_shape=jax.ShapeDtypeStruct((rhs, points), f32),
        in_specs=[SM] + [VM] * 4,
        out_specs=VM,
        scratch_shapes=[
            pltpu.VMEM((wide, rhs, 128), bf16),
            pltpu.VMEM((wide, 8, 128), f32),
            pltpu.VMEM((wide, 8, 128), f32),
            pltpu.VMEM((leaves, 16, 128), bf16),
        ],
        compiler_params=params,
        name="near",
        cost_estimate=pl.CostEstimate(flops=2 * 10**10, bytes_accessed=5 * 10**6, transcendentals=16 * 10**6),
    )(near_index, densities, geometry, left, right)

    return pl.pallas_call(
        functools.partial(down_kernel, shards),
        out_shape=jax.ShapeDtypeStruct((rhs, points), bf16),
        in_specs=[SM] * 4 + [VM] * 14,
        out_specs=VM,
        scratch_shapes=[pltpu.VMEM((3 * nodes, rank, rhs), bf16)],
        compiler_params=params,
        name="down",
        cost_estimate=pl.CostEstimate(flops=10**8, bytes_accessed=5 * 10**6, transcendentals=0),
    )(
        partners_one, partners_two, partners_three, partners_four,
        coefs, cleft, cright, three,
        coupling_one, coupling_two, coupling_three, coupling_four,
        transfer_one, transfer_two, transfer_three, transfer_four,
        leaf_basis, nearf,
    )


def solution(mesh):
    every = ("groups", "leaf", "rhs", "sub")
    split = lambda n: P(every, *([None] * n))
    level = [split(3), split(3), split(1)]
    in_specs = (
        P(None, every), P(None, every), split(1), split(2),
        *level, *level, *level,
        P("groups", None, None, None), P("groups", None, None, None), P("groups", None),
    )
    return jax.shard_map(body, mesh=mesh, in_specs=in_specs, out_specs=P(None, every), check_vma=False)
```

time: 170 us -> 92.4 us (0.54)
  the two profiles are of different devices: /device:TPU:0 before, /device:TPU:1 now
where the time goes in v1:
time: 92.4 us; the launch traced here: 92.1 us
  Pallas kernels  61.3 us (66%)
  blocking collectives  20.7 us (22%)
  starting transfers between devices  5.48 us (6%)
  local copies, waits for them, and re-layouts  2.49 us (3%)
  other arithmetic  1.83 us (2%)
    pallas_call x1, Pallas kernels, body(): pl.pallas_call(functools.partial(near_kernel, shards), out_shape=jax.Shap...  48.4 us
    all_gather x1, blocking collectives, body(): lax.all_gather(coefs[nodes - 1].reshape(1, -1), AXES, axis=0, tiled=True)  20.7 us
    pallas_call x1, Pallas kernels, body(): pl.pallas_call(functools.partial(down_kernel, shards), out_shape=jax.Shap...  11.8 us
    ppermute x4, starting transfers between devices, shift(): lax.ppermute(v, AXES, [(i, (i + step) % count) for i in range(count)])  5.48 us
    slice x2, local copies, waits for them, and re-layouts, body(): head = jnp.concatenate([densities[:, :width], geometry[:, :width]], axis=0)  1.97 us
  transfers between devices with their start and end apart: 4, of which 0 were waited for; matrix products, arithmetic and copies ran while one was open for 2% of the time, Pallas kernels for 54%

profile of v1, /device:TPU:1, one launch (start us, length us, event | category | flops | bytes accessed | tf_op | source)
XLA Modules:
  0.0 92.1 jit_solution(13190239258026592046)
XLA Ops:
  0.0 0.9 fusion.1
  0.9 0.0 copy-start.15
  0.9 0.0 copy-start.14
  1.0 1.1 %fusion = (bf16[64,2048]{1,0:T(8,128)(2,1)S(1)}, bf16[64,2048]{1,0:T(8,128)(2,1)S(1)}) fusion(bf16[64,8192]{1,0:T(8,128)(2,1)} %dens.3), kind=kLoop, calls=%fused_computation.2 | loop fusion | bytes 1048576 | tf_op jit(solution)/shard_map/slice | solution.py:188
  2.0 0.0 copy-start.10
  2.0 0.7 pad_maximum_fusion
  2.8 2.6 %collective-permute-start.2 = (bf16[68,2048]{1,0:T(8,128)(2,1)}, bf16[68,2048]{1,0:T(8,128)(2,1)S(1)}, u32[]{:S(2)}, u32[]{:S(2)}) collective-permute-start(bf16[68,2048]{1,0:T(8,128)(2,1)} %pad_maximum_fusion), channel_id=1, source_target_pairs={{0,1},{1,2},{2,3},{3,4},{4,5},{5,6},{6,7},{7,8},{8,9},{9,10},{10,1... | collective-permute-start | bytes 835592 | tf_op jit(solution)/shard_map/ppermute | solution.py:170
  5.4 0.7 pad_maximum_fusion.1
  6.1 0.0 collective-permute-start.3
  6.2 1.1 %up.1.own = bf16[21,32,64]{2,1,0:T(8,128)(2,1)S(1)} custom-call(bf16[64,8192]{1,0:T(8,128)(2,1)S(1)} %copy-done, bf16[64,32,128]{2,1,0:T(8,128)(2,1)S(1)} %copy-done.1, bf16[16,4,32,32]{3,2,1,0:T(8,128)(2,1)S(1)} %copy-done.2, bf16[4,4,32,32]{3,2,1,0:T(8,128)(2,1)S(1)} %copy-done.3, bf16[1,4,32,32]{3,2,1,0:T(8,128)(2,1)S(1)} %copy-done.5), custom_call_target="tpu_custom_call" | custom-call | flops 100000000 | bytes 2000000 | tf_op jit(solution)/shard_map/up/pallas_call | solution.py:192
  7.3 2.9 %collective-permute-start.1 = (bf16[21,32,64]{2,1,0:T(8,128)(2,1)S(1)}, bf16[21,32,64]{2,1,0:T(8,128)(2,1)S(1)}, u32[]{:S(2)}, u32[]{:S(2)}) collective-permute-start(bf16[21,32,64]{2,1,0:T(8,128)(2,1)S(1)} %up.1.own), channel_id=1, source_target_pairs={{0,15},{1,0},{2,1},{3,2},{4,3},{5,4},{6,5},{7,6},{8,7},{9,8},{10,9... | collective-permute-start | bytes 258056 | tf_op jit(solution)/shard_map/ppermute | solution.py:170
  10.2 0.0 collective-permute-start
  10.2 0.1 copy.23.p1
  10.3 0.1 copy.22.near_index
  10.3 0.1 reshape.4
  10.4 20.7 %all-gather = bf16[16,1,2048]{2,1,0:T(2,128)(2,1)S(1)} all-gather(bf16[1,1,2048]{2,1,0:T(2,128)(2,1)S(1)} %reshape.4), channel_id=1, replica_groups=mesh['groups'=2,'leaf'=4,'rhs'=2,'sub'=2] {'leaf','rhs','sub'}, dimensions={0}, use_global_device_ids=true | all-gather | bytes 69632 | tf_op jit(solution)/shard_map/all_gather | solution.py:204
  31.1 0.4 reduce
  31.5 0.2 reshape.3.three
  31.6 0.0 copy-start.4
  31.7 0.0 copy-start.6
  31.7 0.0 copy-start.7
  31.7 0.0 copy-start.8
  31.7 0.0 copy-start.9
  31.7 0.0 copy-start.11
  31.7 0.0 copy-start.12
  31.7 0.0 copy-start.13
  31.7 0.0 collective-permute-done.2.left
  31.7 0.0 collective-permute-done.3.right
  31.8 48.4 %near.1.nearf = f32[64,8192]{1,0:T(8,128)S(1)} custom-call(s32[64,16]{1,0:T(8,128)S(1)} %copy.22.near_index, bf16[64,8192]{1,0:T(8,128)(2,1)S(1)} %copy-done, bf16[4,8192]{1,0:T(4,128)(2,1)S(1)} %copy-done.10, bf16[68,2048]{1,0:T(8,128)(2,1)S(1)} %collective-permute-done.2.left, bf16[68,2048]{1,0:T(8,128)(2,1)} %collective-permute-done.3.right), custom_call_target="tpu_custom_call" | custom-call | flops 20000000000 | bytes 5000000 | tf_op jit(solution)/shard_map/near/pallas_call | solution.py:208
  80.2 0.0 collective-permute-done.1.right
  80.2 0.0 collective-permute-done.left
  80.3 11.8 %down.1 = bf16[64,8192]{1,0:T(8,128)(2,1)} custom-call(s32[16,4]{1,0:T(8,128)S(1)} %copy.23.p1, s32[4,4]{1,0:T(4,128)S(1)} %copy-done.11, s32[1,4]{1,0:T(1,128)S(1)} %copy-done.13, s32[4,4]{1,0:T(4,128)S(1)} %copy-done.12, bf16[21,32,64]{2,1,0:T(8,128)(2,1)S(1)} %up.1.own, bf16[21,32,64]{2,1,0:T(8,128)(2,1)S(1)} %collective-permute-done.left, ...), custom_call_target="tpu_custom_call" | custom-call | flops 100000000 | bytes 5000000 | tf_op jit(solution)/shard_map/down/pallas_call | solution.py:224
  (22 shorter events, 0.0 us)
Async XLA Ops:
  0.0 6.1 %copy-start = (bf16[64,8192]{1,0:T(8,128)(2,1)S(1)}, bf16[64,8192]{1,0:T(8,128)(2,1)}, u32[]{:S(2)}) copy-start(bf16[64,8192]{1,0:T(8,128)(2,1)} %dens.3) | copy-start | bytes 3145732
  0.0 6.1 %copy-start.5 = (bf16[1,4,32,32]{3,2,1,0:T(8,128)(2,1)S(1)}, bf16[1,4,32,32]{3,2,1,0:T(8,128)(2,1)}, u32[]{:S(2)}) copy-start(bf16[1,4,32,32]{3,2,1,0:T(8,128)(2,1)} %t3.3) | copy-start | bytes 24580
  0.0 6.1 %copy-start.3 = (bf16[4,4,32,32]{3,2,1,0:T(8,128)(2,1)S(1)}, bf16[4,4,32,32]{3,2,1,0:T(8,128)(2,1)}, u32[]{:S(2)}) copy-start(bf16[4,4,32,32]{3,2,1,0:T(8,128)(2,1)} %t2.3) | copy-start | bytes 98308
  0.0 6.1 %copy-start.2 = (bf16[16,4,32,32]{3,2,1,0:T(8,128)(2,1)S(1)}, bf16[16,4,32,32]{3,2,1,0:T(8,128)(2,1)}, u32[]{:S(2)}) copy-start(bf16[16,4,32,32]{3,2,1,0:T(8,128)(2,1)} %t1.3) | copy-start | bytes 393220
  0.0 6.1 %copy-start.1 = (bf16[64,32,128]{2,1,0:T(8,128)(2,1)S(1)}, bf16[64,32,128]{2,1,0:T(8,128)(2,1)}, u32[]{:S(2)}) copy-start(bf16[64,32,128]{2,1,0:T(8,128)(2,1)} %basis.3) | copy-start | bytes 1572868
  0.9 9.2 %copy-start.15 = (s32[16,4]{0,1:T(4,128)S(1)}, s32[16,4]{0,1:T(4,128)}, u32[]{:S(2)}) copy-start(s32[16,4]{0,1:T(4,128)} %param.22) | copy-start | bytes 772
  0.9 9.3 %copy-start.14 = (s32[64,16]{0,1:T(8,128)S(1)}, s32[64,16]{0,1:T(8,128)}, u32[]{:S(2)}) copy-start(s32[64,16]{0,1:T(8,128)} %param.18) | copy-start | bytes 12292
  2.0 29.7 %copy-start.10 = (bf16[4,8192]{1,0:T(4,128)(2,1)S(1)}, bf16[4,8192]{1,0:T(4,128)(2,1)}, u32[]{:S(2)}) copy-start(bf16[4,8192]{1,0:T(4,128)(2,1)} %geom.1) | copy-start | bytes 196612
  2.8 29.0 %collective-permute-start.2 = (bf16[68,2048]{1,0:T(8,128)(2,1)}, bf16[68,2048]{1,0:T(8,128)(2,1)S(1)}, u32[]{:S(2)}, u32[]{:S(2)}) collective-permute-start(bf16[68,2048]{1,0:T(8,128)(2,1)} %pad_maximum_fusion), channel_id=1, source_target_pairs={{0,1},{1,2},{2,3},{3,4},{4,5},{5,6},{6,7},{7,8},{8,9},{9,10},{10,1... | collective-permute-start | bytes 835592 | tf_op jit(solution)/shard_map/ppermute | solution.py:170
  6.1 25.6 %collective-permute-start.3 = (bf16[68,2048]{1,0:T(8,128)(2,1)}, bf16[68,2048]{1,0:T(8,128)(2,1)}, u32[]{:S(2)}, u32[]{:S(2)}) collective-permute-start(bf16[68,2048]{1,0:T(8,128)(2,1)} %pad_maximum_fusion.1), channel_id=1, source_target_pairs={{0,15},{1,0},{2,1},{3,2},{4,3},{5,4},{6,5},{7,6},{8,7},{9,8},{10,9... | collective-permute-start | bytes 835592 | tf_op jit(solution)/shard_map/ppermute | solution.py:170
  7.3 72.9 %collective-permute-start.1 = (bf16[21,32,64]{2,1,0:T(8,128)(2,1)S(1)}, bf16[21,32,64]{2,1,0:T(8,128)(2,1)S(1)}, u32[]{:S(2)}, u32[]{:S(2)}) collective-permute-start(bf16[21,32,64]{2,1,0:T(8,128)(2,1)S(1)} %up.1.own), channel_id=1, source_target_pairs={{0,15},{1,0},{2,1},{3,2},{4,3},{5,4},{6,5},{7,6},{8,7},{9,8},{10,9... | collective-permute-start | bytes 258056 | tf_op jit(solution)/shard_map/ppermute | solution.py:170
  10.2 70.0 %collective-permute-start = (bf16[21,32,64]{2,1,0:T(8,128)(2,1)S(1)}, bf16[21,32,64]{2,1,0:T(8,128)(2,1)S(1)}, u32[]{:S(2)}, u32[]{:S(2)}) collective-permute-start(bf16[21,32,64]{2,1,0:T(8,128)(2,1)S(1)} %up.1.own), channel_id=1, source_target_pairs={{0,1},{1,2},{2,3},{3,4},{4,5},{5,6},{6,7},{7,8},{8,9},{9,10},{10,1... | collective-permute-start | bytes 258056 | tf_op jit(solution)/shard_map/ppermute | solution.py:170
  31.6 48.6 %copy-start.4 = (bf16[16,4,32,32]{3,2,1,0:T(8,128)(2,1)S(1)}, bf16[16,4,32,32]{3,2,1,0:T(8,128)(2,1)}, u32[]{:S(2)}) copy-start(bf16[16,4,32,32]{3,2,1,0:T(8,128)(2,1)} %c1.1) | copy-start | bytes 393220
  31.7 48.6 %copy-start.6 = (bf16[4,4,32,32]{3,2,1,0:T(8,128)(2,1)S(1)}, bf16[4,4,32,32]{3,2,1,0:T(8,128)(2,1)}, u32[]{:S(2)}) copy-start(bf16[4,4,32,32]{3,2,1,0:T(8,128)(2,1)} %c2.1) | copy-start | bytes 98308
  31.7 48.5 %copy-start.7 = (bf16[4,4,32,32]{3,2,1,0:T(8,128)(2,1)S(1)}, bf16[4,4,32,32]{3,2,1,0:T(8,128)(2,1)}, u32[]{:S(2)}) copy-start(bf16[4,4,32,32]{3,2,1,0:T(8,128)(2,1)} %c4.1) | copy-start | bytes 98308
  31.7 48.5 %copy-start.8 = (bf16[4,4,32,32]{3,2,1,0:T(8,128)(2,1)S(1)}, bf16[4,4,32,32]{3,2,1,0:T(8,128)(2,1)}, u32[]{:S(2)}) copy-start(bf16[4,4,32,32]{3,2,1,0:T(8,128)(2,1)} %t4.1) | copy-start | bytes 98308
  31.7 48.5 %copy-start.9 = (bf16[1,4,32,32]{3,2,1,0:T(8,128)(2,1)S(1)}, bf16[1,4,32,32]{3,2,1,0:T(8,128)(2,1)}, u32[]{:S(2)}) copy-start(bf16[1,4,32,32]{3,2,1,0:T(8,128)(2,1)} %c3.1) | copy-start | bytes 24580
  31.7 48.5 %copy-start.11 = (s32[4,4]{1,0:T(4,128)S(1)}, s32[4,4]{1,0:T(4,128)}, u32[]{:S(2)}) copy-start(s32[4,4]{1,0:T(4,128)} %p2.1) | copy-start | bytes 196
  31.7 48.5 %copy-start.12 = (s32[4,4]{1,0:T(4,128)S(1)}, s32[4,4]{1,0:T(4,128)}, u32[]{:S(2)}) copy-start(s32[4,4]{1,0:T(4,128)} %p4.1) | copy-start | bytes 196
  31.7 48.5 %copy-start.13 = (s32[1,4]{1,0:T(1,128)S(1)}, s32[1,4]{1,0:T(1,128)}, u32[]{:S(2)}) copy-start(s32[1,4]{1,0:T(1,128)} %p3.1) | copy-start | bytes 52

commit v2 on v1

v2 whole, which is shorter than its diff:
```python
import functools

import jax
import jax.numpy as jnp
from jax import lax
from jax.experimental import pallas as pl
from jax.experimental.pallas import tpu as pltpu
from jax.sharding import PartitionSpec as P

AXES = ("leaf", "rhs", "sub")
REACH = 16
FAR = 11
SPACING2 = 0.01
SMOOTH = 0.0025
GROUP = 2
FLIP = False
UNROLL = 8
f32 = jnp.float32
bf16 = jnp.bfloat16


def dot(a, b, ca, cb):
    return lax.dot_general(a, b, (((ca,), (cb,)), ((), ())), preferred_element_type=f32)


def wrap(d, total):
    d = jnp.where(d >= total // 2, d - total, d)
    return jnp.where(d < -(total // 2), d + total, d)


def split3(v):
    hi = v.astype(bf16).astype(f32)
    r1 = v - hi
    mid = r1.astype(bf16).astype(f32)
    return r1, r1 - mid


def peers(shards):
    if shards <= 2 * FAR + 1:
        return list(range(1, shards)), shards
    return [d for d in range(-FAR, FAR + 1) if d], 2 * FAR + 1


def slot_of(d, shards):
    if shards <= 2 * FAR + 1:
        return d % shards
    return d + FAR


def exchange_kernel(
    shards, rhs_axis, sub_axis,
    dens, geom, basis, t1, t2, t3,
    own, cleft, cright, three, dleft, dright, gleft, gright,
    c0, stage, send, recv,
):
    leaves = basis.shape[0]
    n1, n2 = t1.shape[0], t2.shape[0]
    nodes = own.shape[0]
    width = dleft.shape[1]
    points = dens.shape[1]
    me = lax.axis_index(AXES)
    offsets, _ = peers(shards)

    def at(step):
        s = lax.rem(me + step + shards, shards)
        return {
            "leaf": s // (rhs_axis * sub_axis),
            "rhs": (s // sub_axis) % rhs_axis,
            "sub": s % sub_axis,
        }

    def copy(src, dst, index, step):
        return pltpu.make_async_remote_copy(
            src_ref=src, dst_ref=dst, send_sem=send.at[index], recv_sem=recv.at[index],
            device_id=at(step), device_id_type=pl.DeviceIdType.MESH,
        )

    barrier = pltpu.get_barrier_semaphore()
    for d in offsets:
        pl.semaphore_signal(barrier, inc=1, device_id=at(d), device_id_type=pl.DeviceIdType.MESH)
    stage[...] = jnp.zeros_like(stage)
    stage[0, 0:4] = geom[:, points - width :]
    stage[1, 0:4] = geom[:, :width]
    pl.semaphore_wait(barrier, len(offsets))

    copies = [
        copy(dens.at[:, pl.ds(points - width, width)], dleft, 0, 1),
        copy(dens.at[:, pl.ds(0, width)], dright, 1, -1),
        copy(stage.at[0], gleft, 2, 1),
        copy(stage.at[1], gright, 3, -1),
    ]
    for c in copies:
        c.start()

    def leaf_coefs(g, carry):
        for u in range(16):
            i = g * 16 + u
            cols = pl.ds(pl.multiple_of(i * 128, 128), 128)
            c0[i] = dot(dens[:, cols], basis[i], 1, 1).astype(bf16)
        return carry

    lax.fori_loop(0, leaves // 16, leaf_coefs, 0)

    def lift(t, n, source, base, into):
        acc = None
        for q in range(4):
            term = dot(source[base + 4 * n + q], t[n, q], 1, 1)
            acc = term if acc is None else acc + term
        own[into + n] = acc.astype(bf16)

    for n in range(n1):
        lift(t1, n, c0, 0, 0)
    for n in range(n2):
        lift(t2, n, own, 0, n1)
    lift(t3, 0, own, n1, n1 + n2)

    more = [copy(own.at[nodes - 1], three.at[slot_of(-d, shards)], 6 + x, d) for x, d in enumerate(offsets)]
    more += [copy(own, cleft, 4, 1), copy(own, cright, 5, -1)]
    for c in more:
        c.start()
    three[slot_of(0, shards)] = own[nodes - 1]
    for c in more + copies:
        c.wait()


def main_kernel(
    shards, near_index, p1, p2, p3, p4,
    dens, geom, dleft, dright, gleft, gright,
    own, cleft, cright, three,
    c1, c2, c3, c4, t1, t2, t3, t4, basis,
    out, wide, densw, fa, fb, tf, grade,
):
    leaves = near_index.shape[0]
    near = near_index.shape[1]
    total = leaves * shards
    me = lax.axis_index(AXES)
    n1, n2 = c1.shape[0], c2.shape[0]

    spans = ((0, n1), (n1, n2), (n1 + n2, 1))
    bases = (0, 3 * n1, 3 * (n1 + n2))
    for (lo, n), base in zip(spans, bases):
        for m in range(n):
            wide[base + m] = cleft[lo + m]
            wide[base + n + m] = own[lo + m]
            wide[base + 2 * n + m] = cright[lo + m]

    def couple(c, p, level, n):
        count = spans[level][1]
        acc = None
        for k in range(4):
            o = wrap(p[n, k] - (me * count + n), count * shards)
            term = dot(wide[bases[level] + count + n + o], c[n, k], 1, 1)
            acc = term if acc is None else acc + term
        return acc

    node = me // 4
    field4 = None
    for k in range(4):
        q4 = p4[node, k]
        acc = None
        for q in range(4):
            d = wrap(4 * q4 + q - me, shards)
            slot = jnp.where(d < 0, d + shards, d) if shards <= 2 * FAR + 1 else d + FAR
            term = dot(three[slot], t4[q4, q], 1, 1)
            acc = term if acc is None else acc + term
        term = dot(acc.astype(bf16), c4[node, k], 1, 1)
        field4 = term if field4 is None else field4 + term
    g4 = field4.astype(bf16)
    g3 = (couple(c3, p3, 2, 0) + dot(g4, t4[node, me % 4], 1, 0)).astype(bf16)
    f2 = [couple(c2, p2, 1, m) for m in range(n2)]
    f1 = [couple(c1, p1, 0, n) for n in range(n1)]
    g2 = [(f2[m] + dot(g3, t3[0, m], 1, 0)).astype(bf16) for m in range(n2)]
    for n in range(n1):
        grade[n] = (f1[n] + dot(g2[n // 4], t2[n // 4, n % 4], 1, 0)).astype(bf16)

    row8 = lax.broadcasted_iota(jnp.int32, (8, 128), 0)
    first = (row8 == 0) | (row8 == 3) | (row8 >= 6)
    second = (row8 == 1) | (row8 == 4)

    def prepare(slot, d, g, mine):
        g = g.astype(f32)
        a, y, z, w = (g[r : r + 1] for r in range(4))
        densw[slot] = (d.astype(f32) * w).astype(bf16)
        a8, y8, z8 = (jnp.broadcast_to(v, (8, 128)) for v in (a, y, z))
        square = SPACING2 * a8 * a8 + y8 * y8 + z8 * z8
        fa[slot] = jnp.where(
            row8 < 3, square + SMOOTH,
            jnp.where(row8 < 6, (-2.0 * SPACING2) * a8, jnp.where(row8 == 6, -2.0 * y8, -2.0 * z8)),
        )
        fb[slot] = jnp.where(row8 < 3, (2.0 * SPACING2) * a8, jnp.where(row8 < 6, -2.0 * SPACING2, 0.0))
        if mine:
            r1, r2 = split3(square)
            upper = jnp.where(row8 < 3, 1.0, jnp.where(row8 < 6, a8, jnp.where(row8 == 6, y8, z8)))
            lower = jnp.where(row8 == 0, square, jnp.where(row8 == 1, r1, jnp.where(row8 == 2, r2, 0.0)))
            tf[slot - REACH] = jnp.concatenate([upper, lower], axis=0).T.astype(bf16)

    for j in range(REACH):
        cols = slice(j * 128, (j + 1) * 128)
        prepare(j, dleft[:, cols], gleft[:, cols], False)
        prepare(REACH + leaves + j, dright[:, cols], gright[:, cols], False)
    for j in range(leaves):
        cols = slice(j * 128, (j + 1) * 128)
        prepare(REACH + j, dens[:, cols], geom[:, cols], True)

    quad = jnp.where(row8 < 3, SPACING2, 0.0)
    tail = jnp.where(row8 < 3, 1.0, 0.0)

    def source(i, k):
        o = wrap(near_index[i, k] - (me * leaves + i), total)
        pos = i + REACH + o
        of = o.astype(f32)
        v = fa[pos] + of * (fb[pos] + of * quad)
        r1, r2 = split3(v)
        x = jnp.where(first, v, jnp.where(second, r1, r2))
        return jnp.concatenate([x, tail], axis=0).astype(bf16), densw[pos]

    def one(i, carry):
        target = tf[i]
        node1 = i // 4
        g0 = dot(grade[node1], t1[node1, i % 4], 1, 0).astype(bf16)
        far = dot(g0, basis[i], 1, 0)
        acc = None
        for k in range(0, near, GROUP):
            xs, ds = zip(*[source(i, k + u) for u in range(GROUP)])
            dist = dot(target, jnp.concatenate(xs, axis=1), 1, 0)
            block = lax.rsqrt(dist.astype(bf16))
            d = jnp.concatenate(ds, axis=1)
            term = dot(d, block, 1, 1) if FLIP else dot(block, d, 1, 1)
            acc = term if acc is None else acc + term
        nearf = acc if FLIP else acc.T
        out[:, pl.ds(pl.multiple_of(i * 128, 128), 128)] = (nearf + far).astype(bf16)
        return carry

    lax.fori_loop(0, leaves, one, 0, unroll=UNROLL)


VM = pl.BlockSpec(memory_space=pltpu.VMEM)
SM = pl.BlockSpec(memory_space=pltpu.SMEM)


def body(
    densities, geometry, near_index, leaf_basis,
    transfer_one, coupling_one, partners_one,
    transfer_two, coupling_two, partners_two,
    transfer_three, coupling_three, partners_three,
    transfer_four, coupling_four, partners_four,
):
    shards = lax.axis_size(AXES)
    leaves, rank, _ = leaf_basis.shape
    rhs, points = densities.shape
    n1, n2 = transfer_one.shape[0], transfer_two.shape[0]
    nodes = n1 + n2 + 1
    width = REACH * 128
    offsets, slots = peers(shards)
    coef = jax.ShapeDtypeStruct((nodes, rhs, rank), bf16)
    side = jax.ShapeDtypeStruct((rhs, width), bf16)
    sideg = jax.ShapeDtypeStruct((16, width), bf16)

    own, cleft, cright, three, dleft, dright, gleft, gright = pl.pallas_call(
        functools.partial(exchange_kernel, shards, lax.axis_size("rhs"), lax.axis_size("sub")),
        out_shape=(
            coef, coef, coef, jax.ShapeDtypeStruct((slots, rhs, rank), bf16),
            side, side, sideg, sideg,
        ),
        in_specs=[VM] * 6,
        out_specs=(VM,) * 8,
        scratch_shapes=[
            pltpu.VMEM((leaves, rhs, rank), bf16),
            pltpu.VMEM((2, 16, width), bf16),
            pltpu.SemaphoreType.DMA((6 + len(offsets),)),
            pltpu.SemaphoreType.DMA((6 + len(offsets),)),
        ],
        compiler_params=pltpu.CompilerParams(
            vmem_limit_bytes=40 * 2**20, collective_id=0, has_side_effects=True
        ),
        name="exchange",
    )(densities, geometry, leaf_basis, transfer_one, transfer_two, transfer_three)

    wide = leaves + 2 * REACH
    return pl.pallas_call(
        functools.partial(main_kernel, shards),
        out_shape=jax.ShapeDtypeStruct((rhs, points), bf16),
        in_specs=[SM] * 5 + [VM] * 19,
        out_specs=VM,
        scratch_shapes=[
            pltpu.VMEM((3 * nodes, rhs, rank), bf16),
            pltpu.VMEM((wide, rhs, 128), bf16),
            pltpu.VMEM((wide, 8, 128), f32),
            pltpu.VMEM((wide, 8, 128), f32),
            pltpu.VMEM((leaves, 128, 16), bf16),
            pltpu.VMEM((n1, rhs, rank), bf16),
        ],
        compiler_params=pltpu.CompilerParams(vmem_limit_bytes=48 * 2**20),
        name="main",
    )(
        near_index, partners_one, partners_two, partners_three, partners_four,
        densities, geometry, dleft, dright, gleft, gright,
        own, cleft, cright, three,
        coupling_one, coupling_two, coupling_three, coupling_four,
        transfer_one, transfer_two, transfer_three, transfer_four,
        leaf_basis,
    )


def solution(mesh):
    every = ("groups", "leaf", "rhs", "sub")
    split = lambda n: P(every, *([None] * n))
    level = [split(3), split(3), split(1)]
    in_specs = (
        P(None, every), P(None, every), split(1), split(2),
        *level, *level, *level,
        P("groups", None, None, None), P("groups", None, None, None), P("groups", None),
    )
    return jax.shard_map(body, mesh=mesh, in_specs=in_specs, out_specs=P(None, every), check_vma=False)
```

time: 92.4 us -> 68.6 us (0.74)
  blocking collectives: 20.7 us -> 0 us
  local copies, waits for them, and re-layouts: 2.49 us -> 11 us
  starting transfers between devices: 5.48 us -> 0 us
  Pallas kernels: 61.3 us -> 57 us
  other arithmetic: 1.83 us -> 0 us
    all_gather x1 -> x0, blocking collectives: 20.7 us -> none  [body(): lax.all_gather(coefs[nodes - 1].reshape(1, -1), AXES, axis=0, tiled=True)]
    unnamed x35 -> x40, local copies, waits for them, and re-layouts: 0.34 us -> 11 us
    ppermute x4 -> x0, starting transfers between devices: 5.48 us -> none  [shift(): lax.ppermute(v, AXES, [(i, (i + step) % count) for i in range(count)])]
    pallas_call x3 -> x2, Pallas kernels: 61.3 us -> 57 us  [the longest x1 32.4 us: body(): pl.pallas_call(functools.partial(main_kernel, shards), out_shape=jax.Shap...]
    slice x3 -> x0, local copies, waits for them, and re-layouts: 1.98 us -> none  [the longest x2 1.97 us: body(): head = jnp.concatenate([densities[:, :width], geometry[:, :width]], axis=0)]
    concatenate x2 -> x0, other arithmetic: 1.47 us -> none  [the longest x1 0.74 us: body(): jnp.concatenate([densities[:, points - width:], geometry[:, points - widt...]
  transfers between devices with their start and end apart: 4 -> 0, of which waited for: 0 -> 0; matrix products, arithmetic and copies ran while one was open for 2% -> 0% of each run, Pallas kernels for 54% -> 0%
where the time goes in v2:
time: 68.6 us; the launch traced here: 68.1 us
  Pallas kernels  57 us (83%)
  local copies, waits for them, and re-layouts  11 us (16%)
    pallas_call x1, Pallas kernels, body(): pl.pallas_call(functools.partial(main_kernel, shards), out_shape=jax.Shap...  32.4 us
    pallas_call x1, Pallas kernels, body(): pl.pallas_call(functools.partial(exchange_kernel, shards, lax.axis_size('...  24.6 us
    unnamed x40, local copies, waits for them, and re-layouts  11 us

profile of v2, /device:TPU:1, one launch (start us, length us, event | category | flops | bytes accessed | tf_op | source)
XLA Modules:
  0.0 68.1 jit_solution(6152645183679386766)
XLA Ops:
  0.0 0.0 copy-start.11
  0.0 0.8 %copy.18.p1 = s32[16,4]{1,0:T(8,128)S(1)} copy(s32[16,4]{0,1:T(4,128)} %param.22) | data formatting | bytes 512 | tf_op args[6]
  0.8 0.8 %copy.17.near_index = s32[64,16]{1,0:T(8,128)S(1)} copy(s32[64,16]{0,1:T(8,128)} %param.18) | data formatting | bytes 8192 | tf_op args[2]
  1.5 0.0 copy-done.11
  1.5 0.0 copy-start
  1.6 1.2 %copy-done = bf16[64,8192]{1,0:T(8,128)(2,1)S(1)} copy-done((bf16[64,8192]{1,0:T(8,128)(2,1)S(1)}, bf16[64,8192]{1,0:T(8,128)(2,1)}, u32[]{:S(2)}) %copy-start) | copy-done | bytes 1048600
  2.8 0.0 copy-start.2
  2.8 1.0 %copy-done.2 = bf16[64,32,128]{2,1,0:T(8,128)(2,1)S(1)} copy-done((bf16[64,32,128]{2,1,0:T(8,128)(2,1)S(1)}, bf16[64,32,128]{2,1,0:T(8,128)(2,1)}, u32[]{:S(2)}) %copy-start.2) | copy-done | bytes 524312
  3.8 0.0 copy-start.4
  3.8 1.0 %copy-done.4 = bf16[16,4,32,32]{3,2,1,0:T(8,128)(2,1)S(1)} copy-done((bf16[16,4,32,32]{3,2,1,0:T(8,128)(2,1)S(1)}, bf16[16,4,32,32]{3,2,1,0:T(8,128)(2,1)}, u32[]{:S(2)}) %copy-start.4) | copy-done | bytes 131096
  4.9 0.9 %copy-done.7 = bf16[4,4,32,32]{3,2,1,0:T(8,128)(2,1)S(1)} copy-done((bf16[4,4,32,32]{3,2,1,0:T(8,128)(2,1)S(1)}, bf16[4,4,32,32]{3,2,1,0:T(8,128)(2,1)}, u32[]{:S(2)}) %copy-start.7) | copy-done | bytes 32792
  5.8 0.8 %copy-done.9 = bf16[4,8192]{1,0:T(4,128)(2,1)S(1)} copy-done((bf16[4,8192]{1,0:T(4,128)(2,1)S(1)}, bf16[4,8192]{1,0:T(4,128)(2,1)}, u32[]{:S(2)}) %copy-start.9) | copy-done | bytes 65560
  6.6 0.0 copy-start.10
  6.6 0.0 copy-start.15
  6.6 24.6 %exchange.1 = (bf16[21,64,32]{2,1,0:T(8,128)(2,1)S(1)}, bf16[21,64,32]{2,1,0:T(8,128)(2,1)S(1)}, bf16[21,64,32]{2,1,0:T(8,128)(2,1)S(1)}, bf16[16,64,32]{2,1,0:T...) custom-call(bf16[64,8192]{1,0:T(8,128)(2,1)S(1)} %copy-done, ...), custom_call_target="tpu_custom_call" | custom-call | tf_op jit(solution)/shard_map/exchange/pallas_call | solution.py:259
  31.2 0.0 copy-start.17
  31.2 0.0 copy-start.16
  31.2 0.0 copy-start.18
  31.2 0.0 copy-done.1
  31.2 0.0 copy-done.3
  31.3 0.0 copy-done.5
  31.3 0.0 copy-done.8
  31.3 0.0 copy-done.10
  31.3 0.0 copy-done.15
  31.3 0.6 copy-done.17
  31.9 0.0 copy-done.16
  31.9 0.0 copy-done.18
  31.9 1.0 %copy-done.6 = bf16[16,4,32,32]{3,2,1,0:T(8,128)(2,1)S(1)} copy-done((bf16[16,4,32,32]{3,2,1,0:T(8,128)(2,1)S(1)}, bf16[16,4,32,32]{3,2,1,0:T(8,128)(2,1)}, u32[]{:S(2)}) %copy-start.6) | copy-done | bytes 131096
  32.9 0.9 %copy-done.12 = bf16[4,4,32,32]{3,2,1,0:T(8,128)(2,1)S(1)} copy-done((bf16[4,4,32,32]{3,2,1,0:T(8,128)(2,1)S(1)}, bf16[4,4,32,32]{3,2,1,0:T(8,128)(2,1)}, u32[]{:S(2)}) %copy-start.12) | copy-done | bytes 32792
  33.9 0.9 %copy-done.13 = bf16[4,4,32,32]{3,2,1,0:T(8,128)(2,1)S(1)} copy-done((bf16[4,4,32,32]{3,2,1,0:T(8,128)(2,1)S(1)}, bf16[4,4,32,32]{3,2,1,0:T(8,128)(2,1)}, u32[]{:S(2)}) %copy-start.13) | copy-done | bytes 32792
  34.8 0.9 %copy-done.14 = bf16[4,4,32,32]{3,2,1,0:T(8,128)(2,1)S(1)} copy-done((bf16[4,4,32,32]{3,2,1,0:T(8,128)(2,1)S(1)}, bf16[4,4,32,32]{3,2,1,0:T(8,128)(2,1)}, u32[]{:S(2)}) %copy-start.14) | copy-done | bytes 32792
  35.7 32.4 %main.1 = bf16[64,8192]{1,0:T(8,128)(2,1)} custom-call(s32[64,16]{1,0:T(8,128)S(1)} %copy.17.near_index, s32[16,4]{1,0:T(8,128)S(1)} %copy.18.p1, s32[4,4]{1,0:T(4,128)S(1)} %copy-done.16, s32[1,4]{1,0:T(1,128)S(1)} %copy-done.18, s32[4,4]{1,0:T(4,128)S(1)} %copy-done.17, bf16[64,8192]{1,0:T(8,128)(2,1)S(1)} %copy-done.1, bf16[4,8192]{1,0:T(4,128)(2,1)S(1)} %copy-done.10, ...), custom_call_target="tpu_custom_call" | custom-call | tf_op jit(solution)/shard_map/main/pallas_call | solution.py:280
  (10 shorter events, 0.0 us)
Async XLA Ops:
  0.0 1.5 %copy-start.11 = (bf16[1,4,32,32]{3,2,1,0:T(8,128)(2,1)S(1)}, bf16[1,4,32,32]{3,2,1,0:T(8,128)(2,1)}, u32[]{:S(2)}) copy-start(bf16[1,4,32,32]{3,2,1,0:T(8,128)(2,1)} %t3.3) | copy-start | bytes 24580
  1.5 1.2 %copy-start = (bf16[64,8192]{1,0:T(8,128)(2,1)S(1)}, bf16[64,8192]{1,0:T(8,128)(2,1)}, u32[]{:S(2)}) copy-start(bf16[64,8192]{1,0:T(8,128)(2,1)} %dens.3) | copy-start | bytes 3145732
  2.8 1.0 %copy-start.2 = (bf16[64,32,128]{2,1,0:T(8,128)(2,1)S(1)}, bf16[64,32,128]{2,1,0:T(8,128)(2,1)}, u32[]{:S(2)}) copy-start(bf16[64,32,128]{2,1,0:T(8,128)(2,1)} %basis.3) | copy-start | bytes 1572868
  3.8 1.0 %copy-start.4 = (bf16[16,4,32,32]{3,2,1,0:T(8,128)(2,1)S(1)}, bf16[16,4,32,32]{3,2,1,0:T(8,128)(2,1)}, u32[]{:S(2)}) copy-start(bf16[16,4,32,32]{3,2,1,0:T(8,128)(2,1)} %t1.3) | copy-start | bytes 393220
  4.9 0.9 %copy-start.7 = (bf16[4,4,32,32]{3,2,1,0:T(8,128)(2,1)S(1)}, bf16[4,4,32,32]{3,2,1,0:T(8,128)(2,1)}, u32[]{:S(2)}) copy-start(bf16[4,4,32,32]{3,2,1,0:T(8,128)(2,1)} %t2.3) | copy-start | bytes 98308
  5.8 0.8 %copy-start.9 = (bf16[4,8192]{1,0:T(4,128)(2,1)S(1)}, bf16[4,8192]{1,0:T(4,128)(2,1)}, u32[]{:S(2)}) copy-start(bf16[4,8192]{1,0:T(4,128)(2,1)} %geom.3) | copy-start | bytes 196612
  6.6 24.6 %copy-start.1 = (bf16[64,8192]{1,0:T(8,128)(2,1)S(1)}, bf16[64,8192]{1,0:T(8,128)(2,1)}, u32[]{:S(2)}) copy-start(bf16[64,8192]{1,0:T(8,128)(2,1)} %dens.3) | copy-start | bytes 3145732
  6.6 24.6 %copy-start.3 = (bf16[64,32,128]{2,1,0:T(8,128)(2,1)S(1)}, bf16[64,32,128]{2,1,0:T(8,128)(2,1)}, u32[]{:S(2)}) copy-start(bf16[64,32,128]{2,1,0:T(8,128)(2,1)} %basis.3) | copy-start | bytes 1572868
  6.6 24.6 %copy-start.5 = (bf16[16,4,32,32]{3,2,1,0:T(8,128)(2,1)S(1)}, bf16[16,4,32,32]{3,2,1,0:T(8,128)(2,1)}, u32[]{:S(2)}) copy-start(bf16[16,4,32,32]{3,2,1,0:T(8,128)(2,1)} %t1.3) | copy-start | bytes 393220
  6.6 24.7 %copy-start.8 = (bf16[4,4,32,32]{3,2,1,0:T(8,128)(2,1)S(1)}, bf16[4,4,32,32]{3,2,1,0:T(8,128)(2,1)}, u32[]{:S(2)}) copy-start(bf16[4,4,32,32]{3,2,1,0:T(8,128)(2,1)} %t2.3) | copy-start | bytes 98308
  6.6 24.7 %copy-start.10 = (bf16[4,8192]{1,0:T(4,128)(2,1)S(1)}, bf16[4,8192]{1,0:T(4,128)(2,1)}, u32[]{:S(2)}) copy-start(bf16[4,8192]{1,0:T(4,128)(2,1)} %geom.3) | copy-start | bytes 196612
  6.6 24.7 %copy-start.15 = (bf16[1,4,32,32]{3,2,1,0:T(8,128)(2,1)S(1)}, bf16[1,4,32,32]{3,2,1,0:T(8,128)(2,1)}, u32[]{:S(2)}) copy-start(bf16[1,4,32,32]{3,2,1,0:T(8,128)(2,1)} %c3.1) | copy-start | bytes 24580
  31.2 0.7 %copy-start.17 = (s32[4,4]{1,0:T(4,128)S(1)}, s32[4,4]{1,0:T(4,128)}, u32[]{:S(2)}) copy-start(s32[4,4]{1,0:T(4,128)} %p4.1) | copy-start | bytes 196
  31.2 0.7 %copy-start.16 = (s32[4,4]{1,0:T(4,128)S(1)}, s32[4,4]{1,0:T(4,128)}, u32[]{:S(2)}) copy-start(s32[4,4]{1,0:T(4,128)} %p2.1) | copy-start | bytes 196
  31.2 0.7 copy-start.18
  31.9 1.0 %copy-start.6 = (bf16[16,4,32,32]{3,2,1,0:T(8,128)(2,1)S(1)}, bf16[16,4,32,32]{3,2,1,0:T(8,128)(2,1)}, u32[]{:S(2)}) copy-start(bf16[16,4,32,32]{3,2,1,0:T(8,128)(2,1)} %c1.1) | copy-start | bytes 393220
  32.9 0.9 %copy-start.12 = (bf16[4,4,32,32]{3,2,1,0:T(8,128)(2,1)S(1)}, bf16[4,4,32,32]{3,2,1,0:T(8,128)(2,1)}, u32[]{:S(2)}) copy-start(bf16[4,4,32,32]{3,2,1,0:T(8,128)(2,1)} %c2.1) | copy-start | bytes 98308
  33.8 0.9 %copy-start.13 = (bf16[4,4,32,32]{3,2,1,0:T(8,128)(2,1)S(1)}, bf16[4,4,32,32]{3,2,1,0:T(8,128)(2,1)}, u32[]{:S(2)}) copy-start(bf16[4,4,32,32]{3,2,1,0:T(8,128)(2,1)} %c4.1) | copy-start | bytes 98308
  34.8 0.9 %copy-start.14 = (bf16[4,4,32,32]{3,2,1,0:T(8,128)(2,1)S(1)}, bf16[4,4,32,32]{3,2,1,0:T(8,128)(2,1)}, u32[]{:S(2)}) copy-start(bf16[4,4,32,32]{3,2,1,0:T(8,128)(2,1)} %t4.1) | copy-start | bytes 98308

commit v3 on v2

v3 whole, which is shorter than its diff:
```python
import functools

import jax
import jax.numpy as jnp
from jax import lax
from jax.experimental import pallas as pl
from jax.experimental.pallas import tpu as pltpu
from jax.sharding import PartitionSpec as P

AXES = ("leaf", "rhs", "sub")
REACH = 16
FAR = 11
SPACING2 = 0.01
SMOOTH = 0.0025
GROUP = 2
UNROLL = 8
f32 = jnp.float32
bf16 = jnp.bfloat16


def dot(a, b, ca, cb):
    return lax.dot_general(a, b, (((ca,), (cb,)), ((), ())), preferred_element_type=f32)


def wrap(d, total):
    d = jnp.where(d >= total // 2, d - total, d)
    return jnp.where(d < -(total // 2), d + total, d)


def split3(v):
    hi = v.astype(bf16).astype(f32)
    r1 = v - hi
    mid = r1.astype(bf16).astype(f32)
    return r1, r1 - mid


def peers(shards):
    if shards <= 2 * FAR + 1:
        return list(range(1, shards)), shards
    return [d for d in range(-FAR, FAR + 1) if d], 2 * FAR + 1


def slot_of(d, shards):
    if shards <= 2 * FAR + 1:
        return d % shards
    return d + FAR


def whole_kernel(
    shards, rhs_axis, sub_axis,
    near_index, p1, p2, p3, p4,
    dens_hbm, geom_hbm, basis_hbm, t1_hbm, t2_hbm, t3_hbm, t4_hbm, c1_hbm, c2_hbm, c3_hbm, c4_hbm,
    out,
    dens, geom, basis, t1, t2, t3, t4, c1, c2, c3, c4,
    own, cleft, cright, three, dleft, dright, gleft, gright,
    c0, stage, wide, densw, fa, fb, tf, grade, nearf,
    load, send, recv,
):
    leaves = basis.shape[0]
    near = near_index.shape[0]
    total = leaves * shards
    n1, n2 = t1.shape[0], t2.shape[0]
    nodes = own.shape[0]
    width = dleft.shape[1]
    points = dens.shape[1]
    me = lax.axis_index(AXES)
    offsets, _ = peers(shards)

    pairs = (
        (dens_hbm, dens), (geom_hbm, geom), (basis_hbm, basis), (t1_hbm, t1), (t2_hbm, t2), (t3_hbm, t3),
        (t4_hbm, t4), (c1_hbm, c1), (c2_hbm, c2), (c3_hbm, c3), (c4_hbm, c4),
    )
    loads = [pltpu.make_async_copy(src, dst, load.at[x]) for x, (src, dst) in enumerate(pairs)]
    for c in loads:
        c.start()

    def at(step):
        s = lax.rem(me + step + shards, shards)
        return {
            "leaf": s // (rhs_axis * sub_axis),
            "rhs": (s // sub_axis) % rhs_axis,
            "sub": s % sub_axis,
        }

    def copy(src, dst, index, step):
        return pltpu.make_async_remote_copy(
            src_ref=src, dst_ref=dst, send_sem=send.at[index], recv_sem=recv.at[index],
            device_id=at(step), device_id_type=pl.DeviceIdType.MESH,
        )

    barrier = pltpu.get_barrier_semaphore()
    for d in offsets:
        pl.semaphore_signal(barrier, inc=1, device_id=at(d), device_id_type=pl.DeviceIdType.MESH)
    stage[...] = jnp.zeros_like(stage)
    loads[0].wait()
    loads[1].wait()
    stage[0, 0:4] = geom[:, points - width :]
    stage[1, 0:4] = geom[:, :width]
    loads[2].wait()

    def leaf_coefs(g, carry):
        for u in range(16):
            i = g * 16 + u
            cols = pl.ds(pl.multiple_of(i * 128, 128), 128)
            c0[i] = dot(dens[:, cols], basis[i], 1, 1).astype(bf16)
        return carry

    lax.fori_loop(0, leaves // 16, leaf_coefs, 0)
    for c in loads[3:6]:
        c.wait()

    def lift(t, n, source, base, into):
        acc = None
        for q in range(4):
            term = dot(source[base + 4 * n + q], t[n, q], 1, 1)
            acc = term if acc is None else acc + term
        own[into + n] = acc.astype(bf16)

    for n in range(n1):
        lift(t1, n, c0, 0, 0)
    for n in range(n2):
        lift(t2, n, own, 0, n1)
    lift(t3, 0, own, n1, n1 + n2)
    pl.semaphore_wait(barrier, len(offsets))

    halos = [
        copy(dens.at[:, pl.ds(points - width, width)], dleft, 0, 1),
        copy(dens.at[:, pl.ds(0, width)], dright, 1, -1),
        copy(stage.at[0], gleft, 2, 1),
        copy(stage.at[1], gright, 3, -1),
    ]
    more = [copy(own.at[nodes - 1], three.at[slot_of(-d, shards)], 6 + x, d) for x, d in enumerate(offsets)]
    more += [copy(own, cleft, 4, 1), copy(own, cright, 5, -1)]
    for c in halos + more:
        c.start()
    three[slot_of(0, shards)] = own[nodes - 1]

    row8 = lax.broadcasted_iota(jnp.int32, (8, 128), 0)
    first = (row8 == 0) | (row8 == 3) | (row8 >= 6)
    second = (row8 == 1) | (row8 == 4)

    def prepare(slot, d, gb, mine):
        densw[slot] = d * gb[3:4]
        g = gb.astype(f32)
        a8, y8, z8 = (jnp.broadcast_to(g[r : r + 1], (8, 128)) for r in range(3))
        square = SPACING2 * a8 * a8 + y8 * y8 + z8 * z8
        fa[slot] = jnp.where(
            row8 < 3, square + SMOOTH,
            jnp.where(row8 < 6, (-2.0 * SPACING2) * a8, jnp.where(row8 == 6, -2.0 * y8, -2.0 * z8)),
        )
        fb[slot] = jnp.where(row8 < 3, (2.0 * SPACING2) * a8, jnp.where(row8 < 6, -2.0 * SPACING2, 0.0))
        if mine:
            r1, r2 = split3(square)
            upper = jnp.where(row8 < 3, 1.0, jnp.where(row8 < 6, a8, jnp.where(row8 == 6, y8, z8)))
            lower = jnp.where(row8 == 0, square, jnp.where(row8 == 1, r1, jnp.where(row8 == 2, r2, 0.0)))
            tf[slot - REACH] = jnp.concatenate([upper, lower], axis=0).T.astype(bf16)

    def prepare_own(g, carry):
        for u in range(16):
            j = g * 16 + u
            cols = pl.ds(pl.multiple_of(j * 128, 128), 128)
            prepare(REACH + j, dens[:, cols], geom[:, cols], True)
        return carry

    lax.fori_loop(0, leaves // 16, prepare_own, 0)

    quad = jnp.where(row8 < 3, SPACING2, 0.0)
    tail = jnp.where(row8 < 3, 1.0, 0.0)

    def source(i, k):
        o = wrap(near_index[k, i] - (me * leaves + i), total)
        pos = jnp.clip(i + REACH + o, 0, leaves + 2 * REACH - 1)
        of = o.astype(f32)
        v = fa[pos] + of * (fb[pos] + of * quad)
        r1, r2 = split3(v)
        x = jnp.where(first, v, jnp.where(second, r1, r2))
        return jnp.concatenate([x, tail], axis=0).astype(bf16), densw[pos]

    def near_leaf(i):
        target = tf[i]
        acc = None
        for k in range(0, near, GROUP):
            xs, ds = zip(*[source(i, k + u) for u in range(GROUP)])
            dist = dot(target, jnp.concatenate(xs, axis=1), 1, 0)
            block = lax.rsqrt(dist.astype(bf16))
            term = dot(block, jnp.concatenate(ds, axis=1), 1, 1)
            acc = term if acc is None else acc + term
        return acc.T

    def far_leaf(i):
        node1 = i // 4
        g0 = dot(grade[node1], t1[node1, i % 4], 1, 0).astype(bf16)
        return dot(g0, basis[i], 1, 0)

    def inner(g, carry):
        for u in range(UNROLL):
            j = g * UNROLL + u
            nearf[j] = near_leaf(j + REACH)
        return carry

    count = leaves - 2 * REACH
    lax.fori_loop(0, count // UNROLL, inner, 0)

    for c in halos + more:
        c.wait()
    for c in loads[6:]:
        c.wait()
    for j in range(REACH):
        cols = slice(j * 128, (j + 1) * 128)
        prepare(j, dleft[:, cols], gleft[0:4, cols], False)
        prepare(REACH + leaves + j, dright[:, cols], gright[0:4, cols], False)

    spans = ((0, n1), (n1, n2), (n1 + n2, 1))
    bases = (0, 3 * n1, 3 * (n1 + n2))
    for (lo, n), base in zip(spans, bases):
        for m in range(n):
            wide[base + m] = cleft[lo + m]
            wide[base + n + m] = own[lo + m]
            wide[base + 2 * n + m] = cright[lo + m]

    def couple(c, p, level, n):
        cells = spans[level][1]
        acc = None
        for k in range(4):
            o = wrap(p(n, k) - (me * cells + n), cells * shards)
            place = jnp.clip(cells + n + o, 0, 3 * cells - 1)
            term = dot(wide[bases[level] + place], c[n, k], 1, 1)
            acc = term if acc is None else acc + term
        return acc

    node = me // 4
    field4 = None
    for k in range(4):
        q4 = p4[node, k]
        acc = None
        for q in range(4):
            d = wrap(4 * q4 + q - me, shards)
            slot = jnp.where(d < 0, d + shards, d) if shards <= 2 * FAR + 1 else jnp.clip(d + FAR, 0, 2 * FAR)
            term = dot(three[slot], t4[q4, q], 1, 1)
            acc = term if acc is None else acc + term
        term = dot(acc.astype(bf16), c4[node, k], 1, 1)
        field4 = term if field4 is None else field4 + term
    g4 = field4.astype(bf16)
    f3 = couple(c3, lambda n, k: p3[n, k], 2, 0)
    f2 = [couple(c2, lambda n, k: p2[n, k], 1, m) for m in range(n2)]
    f1 = [couple(c1, lambda n, k: p1[k, n], 0, n) for n in range(n1)]
    g3 = (f3 + dot(g4, t4[node, me % 4], 1, 0)).astype(bf16)
    g2 = [(f2[m] + dot(g3, t3[0, m], 1, 0)).astype(bf16) for m in range(n2)]
    for n in range(n1):
        grade[n] = (f1[n] + dot(g2[n // 4], t2[n // 4, n % 4], 1, 0)).astype(bf16)

    def store(i, value):
        out[:, pl.ds(pl.multiple_of(i * 128, 128), 128)] = value.astype(bf16)

    def outer(g, carry):
        for u in range(UNROLL):
            j = g * UNROLL + u
            i = jnp.where(j < REACH, j, j + count)
            store(i, near_leaf(i) + far_leaf(i))
        return carry

    lax.fori_loop(0, 2 * REACH // UNROLL, outer, 0)

    def finish(g, carry):
        for u in range(16):
            j = g * 16 + u
            store(j + REACH, nearf[j] + far_leaf(j + REACH))
        return carry

    lax.fori_loop(0, count // 16, finish, 0)


VM = pl.BlockSpec(memory_space=pltpu.VMEM)
HB = pl.BlockSpec(memory_space=pltpu.HBM)
SM = pl.BlockSpec(memory_space=pltpu.SMEM)


def body(
    densities, geometry, near_index, leaf_basis,
    transfer_one, coupling_one, partners_one,
    transfer_two, coupling_two, partners_two,
    transfer_three, coupling_three, partners_three,
    transfer_four, coupling_four, partners_four,
):
    shards = lax.axis_size(AXES)
    leaves, rank, _ = leaf_basis.shape
    rhs, points = densities.shape
    n1, n2 = transfer_one.shape[0], transfer_two.shape[0]
    nodes = n1 + n2 + 1
    width = REACH * 128
    offsets, slots = peers(shards)
    wide = leaves + 2 * REACH
    arrays = (
        densities, geometry, leaf_basis, transfer_one, transfer_two, transfer_three, transfer_four,
        coupling_one, coupling_two, coupling_three, coupling_four,
    )
    coef = pltpu.VMEM((nodes, rhs, rank), bf16)
    return pl.pallas_call(
        functools.partial(whole_kernel, shards, lax.axis_size("rhs"), lax.axis_size("sub")),
        out_shape=jax.ShapeDtypeStruct((rhs, points), bf16),
        in_specs=[SM] * 5 + [HB] * len(arrays),
        out_specs=VM,
        scratch_shapes=[pltpu.VMEM(v.shape, v.dtype) for v in arrays] + [
            coef, coef, coef,
            pltpu.VMEM((slots, rhs, rank), bf16),
            pltpu.VMEM((rhs, width), bf16),
            pltpu.VMEM((rhs, width), bf16),
            pltpu.VMEM((16, width), bf16),
            pltpu.VMEM((16, width), bf16),
            pltpu.VMEM((leaves, rhs, rank), bf16),
            pltpu.VMEM((2, 16, width), bf16),
            pltpu.VMEM((3 * nodes, rhs, rank), bf16),
            pltpu.VMEM((wide, rhs, 128), bf16),
            pltpu.VMEM((wide, 8, 128), f32),
            pltpu.VMEM((wide, 8, 128), f32),
            pltpu.VMEM((leaves, 128, 16), bf16),
            pltpu.VMEM((n1, rhs, rank), bf16),
            pltpu.VMEM((leaves - 2 * REACH, rhs, 128), f32),
            pltpu.SemaphoreType.DMA((len(arrays),)),
            pltpu.SemaphoreType.DMA((6 + len(offsets),)),
            pltpu.SemaphoreType.DMA((6 + len(offsets),)),
        ],
        compiler_params=pltpu.CompilerParams(
            vmem_limit_bytes=48 * 2**20, collective_id=0, has_side_effects=True
        ),
        name="whole",
    )(near_index.T, partners_one.T, partners_two, partners_three, partners_four, *arrays)


def solution(mesh):
    every = ("groups", "leaf", "rhs", "sub")
    split = lambda n: P(every, *([None] * n))
    level = [split(3), split(3), split(1)]
    in_specs = (
        P(None, every), P(None, every), split(1), split(2),
        *level, *level, *level,
        P("groups", None, None, None), P("groups", None, None, None), P("groups", None),
    )
    return jax.shard_map(body, mesh=mesh, in_specs=in_specs, out_specs=P(None, every), check_vma=False)
```

time: 68.6 us -> 57.1 us (0.83)
  Pallas kernels: 57 us -> 42.4 us
  local copies, waits for them, and re-layouts: 11 us -> 14 us
    pallas_call x2 -> x1, Pallas kernels: 57 us -> 42.4 us  [body(): pl.pallas_call(functools.partial(whole_kernel, shards, lax.axis_size('rhs...]
    unnamed x40 -> x33, local copies, waits for them, and re-layouts: 11 us -> 14 us
where the time goes in v3:
time: 57.1 us; the launch traced here: 56.4 us
  Pallas kernels  42.4 us (74%)
  local copies, waits for them, and re-layouts  14 us (25%)
    pallas_call x1, Pallas kernels, body(): pl.pallas_call(functools.partial(whole_kernel, shards, lax.axis_size('rhs...  42.4 us
    unnamed x33, local copies, waits for them, and re-layouts  14 us

profile of v3, /device:TPU:1, one launch (start us, length us, event | category | flops | bytes accessed | tf_op | source)
XLA Modules:
  0.0 56.4 jit_solution(16351177293428971656)
XLA Ops:
  0.0 0.0 copy-start.12
  0.0 0.0 copy-start.15
  0.0 0.7 %copy-done.12 = s32[16,4]{0,1:T(4,128)S(1)} copy-done((s32[16,4]{0,1:T(4,128)S(1)}, s32[16,4]{0,1:T(4,128)}, u32[]{:S(2)}) %copy-start.12) | copy-done | bytes 280
  0.7 0.0 copy-done.15
  0.7 0.0 copy-start
  0.7 1.2 %copy-done = bf16[64,8192]{1,0:T(8,128)(2,1)S(1)} copy-done((bf16[64,8192]{1,0:T(8,128)(2,1)S(1)}, bf16[64,8192]{1,0:T(8,128)(2,1)}, u32[]{:S(2)}) %copy-start) | copy-done | bytes 1048600
  1.9 0.0 copy-start.1
  1.9 1.0 %copy-done.1 = bf16[64,32,128]{2,1,0:T(8,128)(2,1)S(1)} copy-done((bf16[64,32,128]{2,1,0:T(8,128)(2,1)S(1)}, bf16[64,32,128]{2,1,0:T(8,128)(2,1)}, u32[]{:S(2)}) %copy-start.1) | copy-done | bytes 524312
  3.0 0.0 copy-start.2
  3.0 1.0 %copy-done.2 = bf16[16,4,32,32]{3,2,1,0:T(8,128)(2,1)S(1)} copy-done((bf16[16,4,32,32]{3,2,1,0:T(8,128)(2,1)S(1)}, bf16[16,4,32,32]{3,2,1,0:T(8,128)(2,1)}, u32[]{:S(2)}) %copy-start.2) | copy-done | bytes 131096
  4.0 0.0 copy-start.3
  4.0 1.0 %copy-done.3 = bf16[16,4,32,32]{3,2,1,0:T(8,128)(2,1)S(1)} copy-done((bf16[16,4,32,32]{3,2,1,0:T(8,128)(2,1)S(1)}, bf16[16,4,32,32]{3,2,1,0:T(8,128)(2,1)}, u32[]{:S(2)}) %copy-start.3) | copy-done | bytes 131096
  5.0 0.0 copy-start.4
  5.0 0.9 %copy-done.4 = bf16[4,4,32,32]{3,2,1,0:T(8,128)(2,1)S(1)} copy-done((bf16[4,4,32,32]{3,2,1,0:T(8,128)(2,1)S(1)}, bf16[4,4,32,32]{3,2,1,0:T(8,128)(2,1)}, u32[]{:S(2)}) %copy-start.4) | copy-done | bytes 32792
  5.9 0.0 copy-start.5
  5.9 0.9 %copy-done.5 = bf16[4,4,32,32]{3,2,1,0:T(8,128)(2,1)S(1)} copy-done((bf16[4,4,32,32]{3,2,1,0:T(8,128)(2,1)S(1)}, bf16[4,4,32,32]{3,2,1,0:T(8,128)(2,1)}, u32[]{:S(2)}) %copy-start.5) | copy-done | bytes 32792
  6.8 0.0 copy-start.6
  6.8 0.9 %copy-done.6 = bf16[4,4,32,32]{3,2,1,0:T(8,128)(2,1)S(1)} copy-done((bf16[4,4,32,32]{3,2,1,0:T(8,128)(2,1)S(1)}, bf16[4,4,32,32]{3,2,1,0:T(8,128)(2,1)}, u32[]{:S(2)}) %copy-start.6) | copy-done | bytes 32792
  7.8 0.0 copy-start.7
  7.8 0.9 %copy-done.7 = bf16[4,4,32,32]{3,2,1,0:T(8,128)(2,1)S(1)} copy-done((bf16[4,4,32,32]{3,2,1,0:T(8,128)(2,1)S(1)}, bf16[4,4,32,32]{3,2,1,0:T(8,128)(2,1)}, u32[]{:S(2)}) %copy-start.7) | copy-done | bytes 32792
  8.7 0.8 %copy-done.8 = bf16[4,8192]{1,0:T(4,128)(2,1)S(1)} copy-done((bf16[4,8192]{1,0:T(4,128)(2,1)S(1)}, bf16[4,8192]{1,0:T(4,128)(2,1)}, u32[]{:S(2)}) %copy-start.8) | copy-done | bytes 65560
  9.5 0.8 %copy-done.9 = bf16[1,4,32,32]{3,2,1,0:T(8,128)(2,1)S(1)} copy-done((bf16[1,4,32,32]{3,2,1,0:T(8,128)(2,1)S(1)}, bf16[1,4,32,32]{3,2,1,0:T(8,128)(2,1)}, u32[]{:S(2)}) %copy-start.9) | copy-done | bytes 8216
  10.3 0.0 copy-start.10
  10.3 0.8 %copy-done.10 = bf16[1,4,32,32]{3,2,1,0:T(8,128)(2,1)S(1)} copy-done((bf16[1,4,32,32]{3,2,1,0:T(8,128)(2,1)S(1)}, bf16[1,4,32,32]{3,2,1,0:T(8,128)(2,1)}, u32[]{:S(2)}) %copy-start.10) | copy-done | bytes 8216
  11.0 0.0 copy-start.11
  11.0 0.7 %copy-done.11 = s32[64,16]{0,1:T(8,128)S(1)} copy-done((s32[64,16]{0,1:T(8,128)S(1)}, s32[64,16]{0,1:T(8,128)}, u32[]{:S(2)}) %copy-start.11) | copy-done | bytes 4120
  11.7 0.0 copy-start.13
  11.7 0.7 %copy-done.13 = s32[4,4]{1,0:T(4,128)S(1)} copy-done((s32[4,4]{1,0:T(4,128)S(1)}, s32[4,4]{1,0:T(4,128)}, u32[]{:S(2)}) %copy-start.13) | copy-done | bytes 88
  12.4 0.0 copy-start.14
  12.4 0.7 %copy-done.14 = s32[4,4]{1,0:T(4,128)S(1)} copy-done((s32[4,4]{1,0:T(4,128)S(1)}, s32[4,4]{1,0:T(4,128)}, u32[]{:S(2)}) %copy-start.14) | copy-done | bytes 88
  13.1 42.4 %whole.1 = bf16[64,8192]{1,0:T(8,128)(2,1)S(1)} custom-call(s32[16,64]{1,0:T(8,128)S(1)} %bitcast.2, s32[4,16]{1,0:T(4,128)S(1)} %bitcast.3, s32[4,4]{1,0:T(4,128)S(1)} %copy-done.13, s32[1,4]{1,0:T(1,128)S(1)} %copy-done.15, s32[4,4]{1,0:T(4,128)S(1)} %copy-done.14, bf16[64,8192]{1,0:T(8,128)(2,1)S(1)} %copy-done, bf16[4,8192]{1,0:T(4,128)(2,1)S(1)} %copy-done.8, ...), custom_call_target="tpu_custom_call" | custom-call | tf_op jit(solution)/shard_map/whole/pallas_call | solution.py:298
  55.5 1.0 %copy.18 = bf16[64,8192]{1,0:T(8,128)(2,1)} copy(bf16[64,8192]{1,0:T(8,128)(2,1)S(1)} %whole.1) | data formatting | bytes 2097152
  (2 shorter events, 0.0 us)
Async XLA Ops:
  0.0 0.7 %copy-start.12 = (s32[16,4]{0,1:T(4,128)S(1)}, s32[16,4]{0,1:T(4,128)}, u32[]{:S(2)}) copy-start(s32[16,4]{0,1:T(4,128)} %param.22) | copy-start | bytes 772
  0.0 0.7 %copy-start.15 = (s32[1,4]{1,0:T(1,128)S(1)}, s32[1,4]{1,0:T(1,128)}, u32[]{:S(2)}) copy-start(s32[1,4]{1,0:T(1,128)} %p3.1) | copy-start | bytes 52
  0.7 1.2 %copy-start = (bf16[64,8192]{1,0:T(8,128)(2,1)S(1)}, bf16[64,8192]{1,0:T(8,128)(2,1)}, u32[]{:S(2)}) copy-start(bf16[64,8192]{1,0:T(8,128)(2,1)} %dens_hbm.1) | copy-start | bytes 3145732
  1.9 1.0 %copy-start.1 = (bf16[64,32,128]{2,1,0:T(8,128)(2,1)S(1)}, bf16[64,32,128]{2,1,0:T(8,128)(2,1)}, u32[]{:S(2)}) copy-start(bf16[64,32,128]{2,1,0:T(8,128)(2,1)} %basis_hbm.1) | copy-start | bytes 1572868
  3.0 1.0 %copy-start.2 = (bf16[16,4,32,32]{3,2,1,0:T(8,128)(2,1)S(1)}, bf16[16,4,32,32]{3,2,1,0:T(8,128)(2,1)}, u32[]{:S(2)}) copy-start(bf16[16,4,32,32]{3,2,1,0:T(8,128)(2,1)} %t1_hbm.1) | copy-start | bytes 393220
  4.0 1.0 %copy-start.3 = (bf16[16,4,32,32]{3,2,1,0:T(8,128)(2,1)S(1)}, bf16[16,4,32,32]{3,2,1,0:T(8,128)(2,1)}, u32[]{:S(2)}) copy-start(bf16[16,4,32,32]{3,2,1,0:T(8,128)(2,1)} %c1_hbm.1) | copy-start | bytes 393220
  5.0 0.9 %copy-start.4 = (bf16[4,4,32,32]{3,2,1,0:T(8,128)(2,1)S(1)}, bf16[4,4,32,32]{3,2,1,0:T(8,128)(2,1)}, u32[]{:S(2)}) copy-start(bf16[4,4,32,32]{3,2,1,0:T(8,128)(2,1)} %t2_hbm.1) | copy-start | bytes 98308
  5.9 0.9 %copy-start.5 = (bf16[4,4,32,32]{3,2,1,0:T(8,128)(2,1)S(1)}, bf16[4,4,32,32]{3,2,1,0:T(8,128)(2,1)}, u32[]{:S(2)}) copy-start(bf16[4,4,32,32]{3,2,1,0:T(8,128)(2,1)} %t4_hbm.1) | copy-start | bytes 98308
  6.8 0.9 %copy-start.6 = (bf16[4,4,32,32]{3,2,1,0:T(8,128)(2,1)S(1)}, bf16[4,4,32,32]{3,2,1,0:T(8,128)(2,1)}, u32[]{:S(2)}) copy-start(bf16[4,4,32,32]{3,2,1,0:T(8,128)(2,1)} %c2_hbm.1) | copy-start | bytes 98308
  7.8 0.9 %copy-start.7 = (bf16[4,4,32,32]{3,2,1,0:T(8,128)(2,1)S(1)}, bf16[4,4,32,32]{3,2,1,0:T(8,128)(2,1)}, u32[]{:S(2)}) copy-start(bf16[4,4,32,32]{3,2,1,0:T(8,128)(2,1)} %c4_hbm.1) | copy-start | bytes 98308
  8.7 0.8 %copy-start.8 = (bf16[4,8192]{1,0:T(4,128)(2,1)S(1)}, bf16[4,8192]{1,0:T(4,128)(2,1)}, u32[]{:S(2)}) copy-start(bf16[4,8192]{1,0:T(4,128)(2,1)} %geom_hbm.1) | copy-start | bytes 196612
  9.5 0.8 %copy-start.9 = (bf16[1,4,32,32]{3,2,1,0:T(8,128)(2,1)S(1)}, bf16[1,4,32,32]{3,2,1,0:T(8,128)(2,1)}, u32[]{:S(2)}) copy-start(bf16[1,4,32,32]{3,2,1,0:T(8,128)(2,1)} %t3_hbm.1) | copy-start | bytes 24580
  10.3 0.8 %copy-start.10 = (bf16[1,4,32,32]{3,2,1,0:T(8,128)(2,1)S(1)}, bf16[1,4,32,32]{3,2,1,0:T(8,128)(2,1)}, u32[]{:S(2)}) copy-start(bf16[1,4,32,32]{3,2,1,0:T(8,128)(2,1)} %c3_hbm.1) | copy-start | bytes 24580
  11.0 0.7 %copy-start.11 = (s32[64,16]{0,1:T(8,128)S(1)}, s32[64,16]{0,1:T(8,128)}, u32[]{:S(2)}) copy-start(s32[64,16]{0,1:T(8,128)} %param.18) | copy-start | bytes 12292
  11.7 0.7 %copy-start.13 = (s32[4,4]{1,0:T(4,128)S(1)}, s32[4,4]{1,0:T(4,128)}, u32[]{:S(2)}) copy-start(s32[4,4]{1,0:T(4,128)} %p2.1) | copy-start | bytes 196
  12.4 0.7 %copy-start.14 = (s32[4,4]{1,0:T(4,128)S(1)}, s32[4,4]{1,0:T(4,128)}, u32[]{:S(2)}) copy-start(s32[4,4]{1,0:T(4,128)} %p4.1) | copy-start | bytes 196

commit v4 on v3

--- a/solution.py
+++ b/solution.py
@@ -321,7 +321,7 @@
             pltpu.SemaphoreType.DMA((6 + len(offsets),)),
         ],
         compiler_params=pltpu.CompilerParams(
-            vmem_limit_bytes=48 * 2**20, collective_id=0, has_side_effects=True
+            vmem_limit_bytes=63 * 2**20, collective_id=0, has_side_effects=True
         ),
         name="whole",
     )(near_index.T, partners_one.T, partners_two, partners_three, partners_four, *arrays)

time: 57.1 us -> 45 us (0.79)
  local copies, waits for them, and re-layouts: 14 us -> 2.26 us
    unnamed x33 -> x1, local copies, waits for them, and re-layouts: 14 us -> 2.26 us
where the time goes in v4:
time: 45 us; the launch traced here: 44.7 us
  Pallas kernels  42.5 us (94%)
  local copies, waits for them, and re-layouts  2.26 us (5%)
    pallas_call x1, Pallas kernels, body(): pl.pallas_call(functools.partial(whole_kernel, shards, lax.axis_size('rhs...  42.5 us
    unnamed x1, local copies, waits for them, and re-layouts  2.26 us

profile of v4, /device:TPU:1, one launch (start us, length us, event | category | flops | bytes accessed | tf_op | source)
XLA Modules:
  0.0 44.7 jit_solution(2860697387854481609)
XLA Ops:
  0.0 42.5 %whole.1 = bf16[64,8192]{1,0:T(8,128)(2,1)} custom-call(s32[16,64]{1,0:T(8,128)} %bitcast.2, s32[4,16]{1,0:T(4,128)} %bitcast.3, s32[4,4]{1,0:T(4,128)} %p2.1, s32[1,4]{1,0:T(1,128)} %p3.1, s32[4,4]{1,0:T(4,128)} %p4.1, bf16[64,8192]{1,0:T(8,128)(2,1)} %dens_hbm.1, bf16[4,8192]{1,0:T(4,128)(2,1)} %geom_hbm.1, bf16[64,32,128]{2,1,0:T(8,128)(2,1)} %basis_hbm.1, ...), custom_call_target="tpu_custom_call" | custom-call | tf_op jit(solution)/shard_map/whole/pallas_call | solution.py:298
  42.5 2.3 %copy.18 = bf16[64,8192]{1,0:T(8,128)(2,1)} copy(bf16[64,8192]{1,0:T(8,128)(2,1)} %whole.1) | data formatting | bytes 2097152
